TPU v7x, 128 devices: a whole 4x4x4 slice. The times are simulated.
128 devices in a mesh: gx: 16 (over y, x), gy: 8 (over z, core).
Axes of the slice: x: 4, y: 4, z: 4, core: 2. Of those that a mesh axis runs over, the one named last changes fastest.
Arguments:
- mentions: bfloat16 [16384, 1024], P(('gx', 'gy')), may hold values from -150 to 150
- centroids: bfloat16 [128, 1024], replicated, may hold values from -6 to 6
- clusters: int32 [16384, 9], P(('gx', 'gy')), may hold values from 0 to 127, all different within a row; in each aligned block of 128 rows (0 to 127, 128 to 255, ...) at most 13 rows name the same one
- gold_entity: int32 [16384], P(('gx', 'gy')), may hold values from 0 to 1023
- cluster_map: int32 [128], replicated, may hold values from 0 to 127, each once
- entities: bfloat16 [128, 1024, 1024], P(('gx', 'gy')), may hold values from -6 to 6
- m_state: float32 [128, 1024, 1024], P(('gx', 'gy')), may hold values from -6 to 6
- v_state: float32 [128, 1024, 1024], P(('gx', 'gy')), may hold values from 0.1 to 2
Outputs:
- losses: float32 [16384], P(('gx', 'gy'))
- mention_grad: float32 [16384, 1024], P(('gx', 'gy'))
- centroid_grad: float32 [128, 1024], P(('gx', 'gy'))
- new_entities: bfloat16 [128, 1024, 1024], P(('gx', 'gy'))
- new_m: float32 [128, 1024, 1024], P(('gx', 'gy'))
- new_v: float32 [128, 1024, 1024], P(('gx', 'gy'))
Inputs may be any that keep to these rules, and one draw needn't show every extreme that they name: Each row names 9 different clusters, the gold one first. Among the mentions of one device no cluster is named more than 13 times, and in every draw some cluster is named exactly 13 times among the mentions of some device. A permutation: cluster c sits at row cluster_map[c] of entities, m_state and v_state.
All inputs are finite; a program needn't handle non-finite values.
Results may differ from a plain program's by a relative error of at most 0.0027.
Values may be sent and summed in bfloat16 or wider, within the bound.
A program may use at most 128 MiB of HBM per device.

v0:
```python
import math

import jax
import jax.numpy as jnp
from jax import lax
from jax.sharding import PartitionSpec as P

BETA_ONE = 0.9
BETA_TWO = 0.999
STEP_SIZE = 0.05
EPSILON = 1e-08


def earlier_count(slot_ids):
    count = slot_ids.shape[0]
    order = jnp.arange(count, dtype=jnp.int32)
    earlier = (slot_ids[None, :] == slot_ids[:, None]) & (order[None, :] < order[:, None])
    return jnp.sum(earlier.astype(jnp.int32), axis=1)


def body(mentions, centroids, clusters, gold_entity, cluster_map, entities, m_state, v_state):
    rows_here, width = mentions.shape
    picks = clusters.shape[1]
    total_clusters = centroids.shape[0]
    local_clusters, ents_count, _ = entities.shape
    devices = lax.axis_size(("gx", "gy"))
    capacity = 3 * ((rows_here * picks + total_clusters - 1) // total_clusters) // 2
    inverse_root = 1.0 / math.sqrt(width)
    cluster_scores = (
        jnp.dot(mentions, centroids.T, preferred_element_type=jnp.float32) * inverse_root
    )
    cluster_norm = jax.nn.logsumexp(cluster_scores, axis=1)
    gold_hot = (jnp.arange(total_clusters, dtype=jnp.int32)[None, :] == clusters[:, 0:1]).astype(
        jnp.float32
    )
    cluster_gold = jnp.sum(cluster_scores * gold_hot, axis=1)
    cluster_coef = (jnp.exp(cluster_scores - cluster_norm[:, None]) - gold_hot).astype(jnp.bfloat16)
    direct_grad = (
        jnp.dot(cluster_coef, centroids, preferred_element_type=jnp.float32) * inverse_root
    )
    centroid_grad = lax.psum_scatter(
        lax.dot_general(
            cluster_coef, mentions, (((0,), (0,)), ((), ())), preferred_element_type=jnp.float32
        )
        * inverse_root,
        ("gx", "gy"),
        scatter_dimension=0,
        tiled=True,
    )
    pair_total = rows_here * picks
    pair_ids = jnp.arange(pair_total, dtype=jnp.int32)
    slot_ids = jnp.take(cluster_map, clusters.reshape(-1))
    destinations = slot_ids * capacity + earlier_count(slot_ids)
    mention_of = pair_ids // picks
    tag_value = jnp.where(pair_ids % picks == 0, gold_entity[mention_of] + 1, 0)
    pair_tags = jnp.stack([tag_value // 64, tag_value % 64], axis=1).astype(jnp.bfloat16)
    buffer_rows = total_clusters * capacity
    send_rows = (
        jnp.zeros((buffer_rows, width), jnp.bfloat16).at[destinations].set(mentions[mention_of])
    )
    send_tags = jnp.zeros((buffer_rows, 2), jnp.bfloat16).at[destinations].set(pair_tags)
    arrived, arrived_tags = (
        lax.all_to_all(send_rows, ("gx", "gy"), split_axis=0, concat_axis=0, tiled=True),
        lax.all_to_all(send_tags, ("gx", "gy"), split_axis=0, concat_axis=0, tiled=True),
    )
    arrived = arrived.reshape(devices, local_clusters, capacity, width)
    arrived_tags = arrived_tags.reshape(devices, local_clusters, capacity, 2).astype(jnp.float32)
    tag_number = arrived_tags[..., 0] * 64.0 + arrived_tags[..., 1]
    scores = (
        jnp.einsum("skmd,ked->skme", arrived, entities, preferred_element_type=jnp.float32)
        * inverse_root
    )
    partial_norm = jax.nn.logsumexp(scores, axis=-1)
    positions = jnp.arange(ents_count, dtype=jnp.float32) + 1.0
    hits = (positions == tag_number[..., None]).astype(jnp.float32)
    partial_gold = jnp.sum(scores * hits, axis=-1)
    norm_back, gold_back = (
        lax.all_to_all(
            partial_norm.reshape(-1), ("gx", "gy"), split_axis=0, concat_axis=0, tiled=True
        ),
        lax.all_to_all(
            partial_gold.reshape(-1), ("gx", "gy"), split_axis=0, concat_axis=0, tiled=True
        ),
    )
    pair_norm = norm_back[destinations].reshape(rows_here, picks)
    entity_norm = jax.nn.logsumexp(pair_norm, axis=1)
    entity_gold = gold_back[destinations].reshape(rows_here, picks)[:, 0]
    losses = cluster_norm - cluster_gold + entity_norm - entity_gold
    total_send = (
        jnp.zeros((buffer_rows,), jnp.float32).at[destinations].set(jnp.repeat(entity_norm, picks))
    )
    totals = lax.all_to_all(
        total_send, ("gx", "gy"), split_axis=0, concat_axis=0, tiled=True
    ).reshape(devices, local_clusters, capacity)
    entity_coef = (jnp.exp(scores - totals[..., None]) - hits).astype(jnp.bfloat16)
    entity_grad = (
        jnp.einsum("skme,skmd->ked", entity_coef, arrived, preferred_element_type=jnp.float32)
        * inverse_root
    )
    returned = (
        jnp.einsum("skme,ked->skmd", entity_coef, entities, preferred_element_type=jnp.float32)
        * inverse_root
    ).astype(jnp.bfloat16)
    coming_back = lax.all_to_all(
        returned.reshape(buffer_rows, width), ("gx", "gy"), split_axis=0, concat_axis=0, tiled=True
    )
    picked = coming_back[destinations].astype(jnp.float32).reshape(rows_here, picks, width)
    mention_grad = direct_grad + jnp.sum(picked, axis=1)
    new_m = BETA_ONE * m_state + (1.0 - BETA_ONE) * entity_grad
    new_v = BETA_TWO * v_state + (1.0 - BETA_TWO) * entity_grad * entity_grad
    new_entities = (
        entities.astype(jnp.float32) - STEP_SIZE * new_m / (jnp.sqrt(new_v) + EPSILON)
    ).astype(jnp.bfloat16)
    return (losses, mention_grad, centroid_grad, new_entities, new_m, new_v)


def solution(mesh):
    placed = (
        P(("gx", "gy"), None),
        P(),
        P(("gx", "gy"), None),
        P(("gx", "gy")),
        P(),
        P(("gx", "gy"), None, None),
        P(("gx", "gy"), None, None),
        P(("gx", "gy"), None, None),
    )
    return jax.shard_map(
        body,
        mesh=mesh,
        in_specs=placed,
        out_specs=(
            P(("gx", "gy")),
            P(("gx", "gy"), None),
            P(("gx", "gy"), None),
            P(("gx", "gy"), None, None),
            P(("gx", "gy"), None, None),
            P(("gx", "gy"), None, None),
        ),
        check_vma=False,
    )
```

profile of v0, /device:TPU:1, one launch (start us, length us, event | category | flops | bytes accessed | tf_op | source)
XLA Modules:
  0.0 442.8 jit_solution(15912833112891158081)
XLA Ops:
  7.2 0.8 copy.47
  8.0 0.2 reshape.416
  8.2 0.2 reshape.417
  8.5 0.1 fusion.23
  8.6 7.0 %gather_fusion = s32[1152]{0:T(1024)S(1)} fusion(s32[128]{0:T(128)S(1)} %copy-done.1, s32[2048]{0:T(1024)S(1)} %pad_clamp_fusion.2), kind=kCustom, calls=%fused_computation | custom fusion | bytes 13824 | tf_op jit(solution)/shard_map/jit(_take)/gather | solution.py:52
  15.6 0.6 convert_reduce_fusion
  16.2 7.0 %gather_fusion.2 = s32[1152]{0:T(1024)S(1)} fusion(s32[128]{0:T(128)S(1)} %copy-done.2, s32[2048]{0:T(1024)S(1)} %pad_clamp_fusion.1), kind=kCustom, calls=%fused_computation.3 | custom fusion | bytes 13824 | tf_op jit(solution)/shard_map/gather | solution.py:55
  23.2 0.1 fusion.25
  23.3 0.2 copy.51
  23.5 6.3 %scatter_custom_fusion.1 = bf16[1664,2]{1,0:T(8,128)(2,1)S(1)} fusion(s32[1152]{0:T(1024)S(1)} %fusion.22, bf16[1152,2]{1,0:T(8,128)(2,1)S(1)} %copy.51, bf16[]{:T(256)} %constant.47.clone.1), kind=kCustom, calls=%fused_computation.45 | custom fusion | bytes 6658 | tf_op jit(solution)/shard_map/scatter | solution.py:61
  29.8 0.2 copy.52
  30.0 0.2 all_to_all.42
  30.3 0.7 copy.53
  31.0 12.1 %all-to-all-start.2 = ((bf16[128,13,2]{1,2,0:T(2,128)(2,1)}), bf16[128,13,2]{1,2,0:T(2,128)(2,1)S(1)}, u32[]{:S(2)}, u32[]{:S(2)}) async-start(bf16[128,13,2]{1,2,0:T(2,128)(2,1)} %copy.53), calls=%async_computation.2 | async-start | bytes 131072 | tf_op jit(solution)/shard_map/all_to_all | solution.py:64
  43.1 21.9 %scatter_custom_fusion = bf16[1664,1024]{1,0:T(8,128)(2,1)} fusion(s32[1152]{0:T(1024)S(1)} %fusion.22, bf16[128,1024]{1,0:T(8,128)(2,1)S(1)} %copy-done, s32[2048]{0:T(1024)S(1)} %pad_clamp_fusion.1, bf16[]{:T(256)} %constant.47.clone.1), kind=kCustom, calls=%fused_computation.36 | custom fusion | bytes 3407874 | tf_op jit(solution)/shard_map/scatter | solution.py:59
  65.0 5.8 %all_to_all.38 = bf16[128,13,1024]{2,1,0:T(8,128)(2,1)} reshape(bf16[1664,1024]{1,0:T(8,128)(2,1)} %scatter_custom_fusion) | data formatting | bytes 6815744 | tf_op jit(solution)/shard_map/all_to_all | solution.py:63
  70.8 10.6 %all-to-all-start = ((bf16[128,13,1024]{2,1,0:T(8,128)(2,1)}), bf16[128,13,1024]{2,1,0:T(8,128)(2,1)}, u32[]{:S(2)}, u32[]{:S(2)}) async-start(bf16[128,13,1024]{2,1,0:T(8,128)(2,1)} %all_to_all.38), calls=%async_computation | async-start | bytes 8388608 | tf_op jit(solution)/shard_map/all_to_all | solution.py:63
  81.4 0.2 fusion.31
  81.7 0.7 slice_bitcast_fusion
  82.5 0.1 slice_add_fusion
  82.6 0.1 copy.54
  82.6 51.2 %all-to-all-done = bf16[128,13,1024]{2,1,0:T(8,128)(2,1)} async-done(((bf16[128,13,1024]{2,1,0:T(8,128)(2,1)}), bf16[128,13,1024]{2,1,0:T(8,128)(2,1)}, u32[]{:S(2)}, u32[]{:S(2)}) %all-to-all-start) | async-done | bytes 3407904 | tf_op jit(solution)/shard_map/all_to_all | solution.py:63
  133.9 9.3 %bitcast_reduce_fusion = (f32[128,13]{0,1:T(8,128)S(1)}, f32[128,13,1024]{2,0,1:T(8,128)S(1)}) fusion(bf16[1,1024,1024]{2,1,0:T(8,128)(2,1)} %param.13, bf16[128,13,1024]{2,1,0:T(8,128)(2,1)} %all-to-all-done), kind=kOutput, calls=%fused_computation.16 | convolution fusion | flops 3493067264 | bytes 12327424 | tf_op jit(solution)/shard_map/skmd,ked->skme/dot_general | solution.py:70
  143.2 2.8 copy-done.3
  146.0 3.0 fusion.4
  149.0 0.7 copy.50
  149.7 4.6 %all-to-all-start.1 = ((f32[128,13,1]{1,2,0:T(1,128)}), f32[128,13,1]{1,2,0:T(1,128)S(1)}, u32[]{:S(2)}, u32[]{:S(2)}) async-start(f32[128,13,1]{1,2,0:T(1,128)} %copy.50), calls=%async_computation.1 | async-start | bytes 131072 | tf_op jit(solution)/shard_map/all_to_all | solution.py:78
  154.4 0.7 copy.55
  155.1 8.6 %all-to-all-done.1 = f32[128,13,1]{1,2,0:T(1,128)S(1)} async-done(((f32[128,13,1]{1,2,0:T(1,128)}), f32[128,13,1]{1,2,0:T(1,128)S(1)}, u32[]{:S(2)}, u32[]{:S(2)}) %all-to-all-start.1) | async-done | bytes 6688 | tf_op jit(solution)/shard_map/all_to_all | solution.py:78
  163.7 4.9 %all-to-all-start.3 = ((f32[128,13,1]{1,2,0:T(1,128)}), f32[128,13,1]{1,2,0:T(1,128)S(1)}, u32[]{:S(2)}, u32[]{:S(2)}) async-start(f32[128,13,1]{1,2,0:T(1,128)} %copy.55), calls=%async_computation.3 | async-start | bytes 131072 | tf_op jit(solution)/shard_map/all_to_all | solution.py:81
  168.6 0.5 broadcast.468
  169.2 0.8 reduce.18
  170.0 0.2 all_to_all.41
  170.2 6.5 %gather_fusion.1 = f32[1152]{0:T(1024)S(1)} fusion(f32[1664]{0:T(1024)S(1)} %all_to_all.41, s32[2048]{0:T(1024)S(1)} %pad_clamp_fusion), kind=kCustom, calls=%fused_computation.2 | custom fusion | bytes 13824 | tf_op jit(solution)/shard_map/gather | solution.py:85
  176.7 0.2 reshape.419
  176.9 0.1 reduce_max.32
  177.0 0.2 exponential_reduce_fusion
  177.2 0.9 all-to-all-done.3
  178.1 0.8 reduce.17
  178.9 0.2 all_to_all.46
  179.1 6.5 %gather_fusion.3 = f32[1152]{0:T(1024)S(1)} fusion(f32[1664]{0:T(1024)S(1)} %all_to_all.46, s32[2048]{0:T(1024)S(1)} %pad_clamp_fusion), kind=kCustom, calls=%fused_computation.4 | custom fusion | bytes 13824 | tf_op jit(solution)/shard_map/gather | solution.py:87
  185.6 0.2 reshape.420
  185.8 0.1 slice_reduce_fusion
  185.9 0.5 add_subtract_fusion
  186.4 0.1 broadcast_in_dim.29
  186.5 0.2 reshape.493
  186.7 6.4 %scatter_custom_fusion.2 = f32[1664]{0:T(1024)S(1)} fusion(s32[1152]{0:T(1024)S(1)} %fusion.22, f32[1152]{0:T(1024)S(1)} %reshape.493, f32[]{:T(128)} %constant.46.clone.1), kind=kCustom, calls=%fused_computation.84 | custom fusion | bytes 6660 | tf_op jit(solution)/shard_map/scatter | solution.py:90
  193.2 0.2 all_to_all.47
  193.4 18.2 %all_to_all.57 = f32[128,13,1]{1,2,0:T(1,128)S(1)} all-to-all(f32[128,13,1]{1,2,0:T(1,128)S(1)} %bitcast.79), channel_id=1, replica_groups=mesh['gx'=16,'gy'=8] {'gx','gy'}, dimensions={0} | all-to-all | bytes 13312 | tf_op jit(solution)/shard_map/all_to_all | solution.py:92
  211.5 0.1 copy.57
  211.6 7.8 %multiply_convert_fusion = bf16[128,13,1024]{2,0,1:T(8,128)(2,1)S(1)} fusion(bf16[1,1024,1024]{2,1,0:T(8,128)(2,1)} %param.13, f32[128,13,1024]{2,0,1:T(8,128)} %copy-done.3, f32[128,13]{0,1:T(8,128)S(1)} %copy.57, f32[128,13]{0,1:T(8,128)S(1)} %copy.54, f32[1024]{0:T(1024)S(1)} %iota_add_fusion), kind=kOutput, calls=%fused_computation.20 | convolution fusion | flops 3503292416 | bytes 12338176 | tf_op jit(solution)/shard_map/skme,ked->skmd/dot_general | solution.py:101
  219.4 4.0 copy.58
  223.4 5.8 %all-to-all-start.5 = ((bf16[128,13,1024]{2,1,0:T(8,128)(2,1)}), bf16[128,13,1024]{2,1,0:T(8,128)(2,1)}, u32[]{:S(2)}, u32[]{:S(2)}) async-start(bf16[128,13,1024]{2,1,0:T(8,128)(2,1)} %copy.58), calls=%async_computation.5 | async-start | bytes 8388608 | tf_op jit(solution)/shard_map/all_to_all | solution.py:104
  229.2 0.3 all-reduce.3.cloned.1.call-start
  229.6 1.0 convolution_multiply_fusion
  230.6 0.0 all-reduce.3.cloned.1.call-update
  230.6 20.6 %subtract_convert_fusion = (bf16[1,1024,1024]{2,1,0:T(8,128)(2,1)}, f32[1,1024,1024]{2,1,0:T(8,128)}, f32[1,1024,1024]{2,1,0:T(8,128)}) fusion(bf16[1,1024,1024]{2,1,0:T(8,128)(2,1)S(1)} %copy-done.5, f32[1,1024,1024]{2,1,0:T(8,128)} %param.14, f32[1,1024,1024]{2,1,0:T(8,128)} %param.15, bf16[128,13,1024]{2,1,0:T(8,128)(2,1)} %all-to-all-done, ...), kind=kOutput, calls=%fused_computation.30 | convolution fusion | flops 3514564608 | bytes 31212544 | tf_op jit(solution)/shard_map/skme,skmd->ked/dot_general | solution.py:97
  251.2 158.0 %all-reduce.3.cloned.1.call-done = f32[128,1024]{1,0:T(8,128)} async-done(((f32[128,1024]{1,0:T(8,128)}), f32[128,1024]{1,0:T(8,128)}) %all-reduce.3.cloned.1.call-update) | async-done | bytes 524304
  409.3 1.4 constant_dynamic-slice_fusion
  410.6 6.2 %all_to_all.50 = bf16[1664,1024]{1,0:T(8,128)(2,1)} reshape(bf16[128,13,1024]{2,1,0:T(8,128)(2,1)} %all-to-all-done.5) | data formatting | bytes 6815744 | tf_op jit(solution)/shard_map/all_to_all | solution.py:104
  416.8 8.5 %gather_fusion.4 = bf16[1152,1024]{1,0:T(8,128)(2,1)S(1)} fusion(bf16[1664,1024]{1,0:T(8,128)(2,1)} %all_to_all.50, s32[2048]{0:T(1024)S(1)} %pad_clamp_fusion), kind=kCustom, calls=%fused_computation.5 | custom fusion | bytes 4723200 | tf_op jit(solution)/shard_map/gather | solution.py:107
  425.3 3.7 reshape.424
  429.0 5.4 %reduce_sum.72 = f32[128,1024]{1,0:T(8,128)S(1)} reduce(f32[128,9,1024]{2,1,0:T(8,128)} %reshape.424, f32[]{:T(128)} %constant.46.clone.1), dimensions={1}, to_apply=%region_12.13 | reduce | flops 1048576 | bytes 5242884 | tf_op jit(solution)/shard_map/reduce_sum | solution.py:108
  434.4 1.1 fusion.18
  (28 shorter events, 0.3 us)
Async XLA Ops:
  7.2 35.9 %copy-start = (bf16[128,1024]{1,0:T(8,128)(2,1)S(1)}, bf16[128,1024]{1,0:T(8,128)(2,1)}, u32[]{:S(2)}) copy-start(bf16[128,1024]{1,0:T(8,128)(2,1)} %param.8) | copy-start | bytes 786436
  7.2 1.4 copy-start.1
  8.6 7.7 %copy-start.2 = (s32[128]{0:T(128)S(1)}, s32[128]{0:T(128)}, u32[]{:S(2)}) copy-start(s32[128]{0:T(128)} %param.11) | copy-start | bytes 1540
  31.0 39.9 %all-to-all-start.2 = ((bf16[128,13,2]{1,2,0:T(2,128)(2,1)}), bf16[128,13,2]{1,2,0:T(2,128)(2,1)S(1)}, u32[]{:S(2)}, u32[]{:S(2)}) async-start(bf16[128,13,2]{1,2,0:T(2,128)(2,1)} %copy.53), calls=%async_computation.2 | async-start | bytes 131072 | tf_op jit(solution)/shard_map/all_to_all | solution.py:64
  70.8 10.6 %copy-start.4 = (bf16[128,1024]{1,0:T(8,128)(2,1)S(1)}, bf16[128,1024]{1,0:T(8,128)(2,1)}, u32[]{:S(2)}) copy-start(bf16[128,1024]{1,0:T(8,128)(2,1)} %param.9) | copy-start | bytes 786436
  70.8 63.0 %all-to-all-start = ((bf16[128,13,1024]{2,1,0:T(8,128)(2,1)}), bf16[128,13,1024]{2,1,0:T(8,128)(2,1)}, u32[]{:S(2)}, u32[]{:S(2)}) async-start(bf16[128,13,1024]{2,1,0:T(8,128)(2,1)} %all_to_all.38), calls=%async_computation | async-start | bytes 8388608 | tf_op jit(solution)/shard_map/all_to_all | solution.py:63
  143.2 2.8 copy-start.3
  149.7 14.0 %all-to-all-start.1 = ((f32[128,13,1]{1,2,0:T(1,128)}), f32[128,13,1]{1,2,0:T(1,128)S(1)}, u32[]{:S(2)}, u32[]{:S(2)}) async-start(f32[128,13,1]{1,2,0:T(1,128)} %copy.50), calls=%async_computation.1 | async-start | bytes 131072 | tf_op jit(solution)/shard_map/all_to_all | solution.py:78
  163.7 14.4 %all-to-all-start.3 = ((f32[128,13,1]{1,2,0:T(1,128)}), f32[128,13,1]{1,2,0:T(1,128)S(1)}, u32[]{:S(2)}, u32[]{:S(2)}) async-start(f32[128,13,1]{1,2,0:T(1,128)} %copy.55), calls=%async_computation.3 | async-start | bytes 131072 | tf_op jit(solution)/shard_map/all_to_all | solution.py:81
  223.4 7.2 %copy-start.5 = (bf16[1,1024,1024]{2,1,0:T(8,128)(2,1)S(1)}, bf16[1,1024,1024]{2,1,0:T(8,128)(2,1)}, u32[]{:S(2)}) copy-start(bf16[1,1024,1024]{2,1,0:T(8,128)(2,1)} %param.13) | copy-start | bytes 6291460
  223.4 187.2 %all-to-all-start.5 = ((bf16[128,13,1024]{2,1,0:T(8,128)(2,1)}), bf16[128,13,1024]{2,1,0:T(8,128)(2,1)}, u32[]{:S(2)}, u32[]{:S(2)}) async-start(bf16[128,13,1024]{2,1,0:T(8,128)(2,1)} %copy.58), calls=%async_computation.5 | async-start | bytes 8388608 | tf_op jit(solution)/shard_map/all_to_all | solution.py:104
  229.2 180.0 %all-reduce.3.cloned.1.call-start = ((), (), s32[]{:S(2)}) async-start(), calls=%async_computation.6 | async-start | bytes 1048576
Sparse Core Ops, SparseCore 0:
  235.4 173.8 all-reduce.2
where the time goes:
time: 448 us; the launch traced here: 443 us
  waiting for transfers between devices  219 us (49%)
  local copies, waits for them, and re-layouts  101 us (23%)
  matrix products  40.1 us (9%)
  starting transfers between devices  38.4 us (9%)
  blocking collectives  18.2 us (4%)
  between operations  14.9 us (3%)
  other arithmetic  11.8 us (3%)
    unnamed x2, waiting for transfers between devices  158 us
    all_to_all x1, waiting for transfers between devices, body(): lax.all_to_all(send_rows, ('gx', 'gy'), split_axis=0, concat_axis=0, tile...  51.2 us
    scatter x1, local copies, waits for them, and re-layouts, body(): jnp.zeros((buffer_rows, width), jnp.bfloat16).at[destinations]  21.9 us
    dot_general x1, matrix products, body(): jnp.einsum('skme,skmd->ked', entity_coef, arrived, preferred_element_type...  20.6 us
    all_to_all x1, blocking collectives, body(): lax.all_to_all(total_send, ('gx', 'gy'), split_axis=0, concat_axis=0, til...  18.2 us
    all_to_all x1, starting transfers between devices, body(): lax.all_to_all(send_tags, ('gx', 'gy'), split_axis=0, concat_axis=0, tile...  12.1 us
    all_to_all x1, starting transfers between devices, body(): lax.all_to_all(send_rows, ('gx', 'gy'), split_axis=0, concat_axis=0, tile...  10.6 us
    dot_general x1, matrix products, body(): jnp.einsum('skmd,ked->skme', arrived, entities, preferred_element_type=jn...  9.33 us
  transfers between devices with their start and end apart: 6, of which 4 were waited for; matrix products, arithmetic and copies ran while one was open for 12% of the time, Pallas kernels for 0%

commit v1 on v0

v1 whole, which is shorter than its diff:
```python
import functools
import math

import jax
import jax.numpy as jnp
from jax import lax
from jax.experimental import pallas as pl
from jax.experimental.pallas import tpu as pltpu
from jax.sharding import PartitionSpec as P

BETA_ONE = 0.9
BETA_TWO = 0.999
STEP_SIZE = 0.05
EPSILON = 1e-08
MESH = pl.DeviceIdType.MESH
SLOTS = 16
MOST = 13
STRIDE = 45
F32 = jnp.float32
BF16 = jnp.bfloat16

NN = (((1,), (0,)), ((), ()))
NT = (((1,), (1,)), ((), ()))
TN = (((0,), (0,)), ((), ()))


def dot(a, b, dims=NN):
    return lax.dot_general(a, b, dims, preferred_element_type=F32)


def iota(shape, dim):
    return lax.broadcasted_iota(jnp.int32, shape, dim)


def kernel(
    n,
    n_gy,
    mentions_ref,
    centroids_ref,
    clusters_ref,
    gold_ref,
    map_ref,
    entities_ref,
    losses_ref,
    mention_grad_ref,
    centroid_grad_ref,
    entity_grad_ref,
    ent,
    snd,
    rcv,
    back,
    scores_ref,
    coef_ref,
    tags_ref,
    parts_ref,
    place_ref,
    gold_place_ref,
    norm_out,
    norm_in,
    total_out,
    total_in,
    ent_sem,
    row_ssem,
    row_rsem,
    norm_ssem,
    norm_rsem,
    total_ssem,
    total_rsem,
    back_ssem,
    back_rsem,
):
    count, width = mentions_ref.shape
    ents = entities_ref.shape[0]
    picks = clusters_ref.shape[1]
    group = 16
    chunks = n // group
    rows = group * SLOTS
    inverse_root = 1.0 / math.sqrt(width)
    gx = lax.axis_index("gx")
    gy = lax.axis_index("gy")
    me = gx * n_gy + gy
    gy_bits = n_gy.bit_length() - 1

    def partner(i):
        k = (i * STRIDE) & (n - 1)
        return (gx ^ lax.shift_right_logical(k, gy_bits), gy ^ (k & (n_gy - 1)))

    barrier = pltpu.get_barrier_semaphore()

    def greet(i, _):
        pl.semaphore_signal(barrier, inc=1, device_id=partner(i), device_id_type=MESH)
        return 0

    lax.fori_loop(1, n, greet, 0)
    ent_copy = pltpu.make_async_copy(entities_ref, ent, ent_sem)
    ent_copy.start()

    def send(src, dst, ssem, rsem, c, j):
        i = c * group + j

        def away():
            pltpu.make_async_remote_copy(
                src_ref=src.at[i],
                dst_ref=dst.at[i],
                send_sem=ssem,
                recv_sem=rsem,
                device_id=partner(i),
                device_id_type=MESH,
            ).start()

        if j == 0:
            pl.when(c > 0)(away)

            @pl.when(c == 0)
            def _():
                pltpu.make_async_copy(src.at[0], dst.at[0], rsem).start()
        else:
            away()

    def await_received(buf, c, sem):
        whole = buf.at[pl.ds(c * group, group)]
        pltpu.make_async_copy(whole, whole, sem).wait()

    def await_sent(buf, c, sem):
        @pl.when(c == 0)
        def _():
            part = buf.at[pl.ds(1, group - 1)]
            pltpu.make_async_copy(part, part, sem).wait()

        @pl.when(c > 0)
        def _():
            await_received(buf, c, sem)

    square = (n, n)
    named = jnp.zeros((count, n), F32)
    for j in range(picks):
        named = named + (clusters_ref[:, j : j + 1] == iota((count, n), 1)).astype(F32)
    gold_named = (clusters_ref[:, 0:1] == iota((count, n), 1)).astype(F32)
    steps = iota(square, 0)
    partners = me ^ ((steps * STRIDE) & (n - 1))
    owner = (partners == iota(square, 1)).astype(BF16)
    row_of = (map_ref[...] == iota(square, 0)).astype(BF16)
    step_of = dot(owner, row_of).astype(BF16)
    here = dot(step_of, named.astype(BF16), NT)
    gold_here = dot(step_of, gold_named.astype(BF16), NT)
    earlier = (iota((count, count), 0) < iota((count, count), 1)).astype(BF16)
    rank = dot(here.astype(BF16), earlier)
    place = jnp.where(here > 0.5, rank, -1.0)
    gold_place = jnp.where(gold_here > 0.5, rank, -1.0)
    place_ref[...] = place
    gold_place_ref[...] = gold_place

    lane = iota((count, 128), 1)
    eye = iota((count, count), 0) == iota((count, count), 1)

    def column(row):
        return jnp.sum(jnp.where(eye, row, 0.0), axis=1, keepdims=True)

    def as_row(col):
        return jnp.sum(jnp.where(eye, col, 0.0), axis=0, keepdims=True)

    def spread(places, parts):
        total = jnp.zeros((n, 128), F32)
        for r in range(MOST):
            values = jnp.zeros((count, 128), F32)
            for p, part in enumerate(parts):
                values = values + jnp.where(lane == 16 * p + r, part, 0.0)
            total = total + dot((places == float(r)).astype(BF16), values.astype(BF16))
        return total

    gold_tag = column((gold_ref[...] + 1).astype(F32))
    tag_high = jnp.floor(gold_tag * (1.0 / 64.0))
    tag_low = gold_tag - 64.0 * tag_high
    tag_rows = spread(gold_place, (tag_high, tag_low)).astype(BF16)
    norm_out[...] = tag_rows.astype(F32).reshape(n, 1, 128)

    sub3 = iota((group, SLOTS, 128), 1)
    lane3 = iota((group, SLOTS, 128), 2)

    def chosen(c):
        places = place_ref[pl.ds(c * group, group), :]
        picked = places[:, None, :] == iota((group, SLOTS, count), 1).astype(F32)
        return picked.astype(F32).reshape(rows, count).astype(BF16)

    put = iota((rows, group), 0) == iota((rows, group), 1) * SLOTS + MOST
    put = put.astype(F32).astype(BF16)

    pl.semaphore_wait(barrier, n - 1)

    def send_rows(c, _):
        block = dot(chosen(c), mentions_ref[...])
        tags = norm_out[pl.ds(c * group, group)].reshape(group, 128).astype(BF16)
        first = block[:, :128] + dot(put, tags)
        slab = snd.at[pl.ds(c * group, group)]
        slab[:, :, 0:128] = first.astype(BF16).reshape(group, SLOTS, 128)
        slab[:, :, 128:] = block[:, 128:].astype(BF16).reshape(group, SLOTS, width - 128)
        for j in range(group):
            send(snd, rcv, row_ssem.at[c], row_rsem.at[c], c, j)
        return 0

    lax.fori_loop(0, chunks, send_rows, 0)

    mentions = mentions_ref[...]
    centroids = centroids_ref[...]
    cluster_scores = dot(mentions, centroids, NT) * inverse_root
    top = jnp.max(cluster_scores, axis=1, keepdims=True)
    cluster_norm = jnp.log(jnp.sum(jnp.exp(cluster_scores - top), axis=1, keepdims=True)) + top
    cluster_gold = jnp.sum(cluster_scores * gold_named, axis=1, keepdims=True)
    cluster_coef = (jnp.exp(cluster_scores - cluster_norm) - gold_named).astype(BF16)
    mention_grad_ref[...] = dot(cluster_coef, centroids) * inverse_root
    shares = dot(cluster_coef, mentions, TN) * inverse_root
    high = shares.astype(BF16)
    low = (shares - high.astype(F32)).astype(BF16)
    parts_ref[0] = dot(owner, high).astype(BF16)
    parts_ref[1] = dot(owner, low).astype(BF16)
    cluster_loss = as_row(cluster_norm - cluster_gold)

    ent_copy.wait()

    tag_weight = jnp.where(lane3 == sub3, 64.0, 0.0) + jnp.where(lane3 == sub3 + 16, 1.0, 0.0)
    norm_lane = (lane3 == sub3).astype(F32)
    gold_lane = (lane3 == sub3 + 16).astype(F32)
    positions = (iota((rows, ents), 1) + 1).astype(F32)

    def score(c, _):
        await_received(rcv, c, row_rsem.at[c])
        block = rcv[pl.ds(c * group, group)]
        scores = dot(block.reshape(rows, width), ent[...], NT) * inverse_root
        tag_row = jnp.sum(
            jnp.where(sub3 == MOST, block[:, :, :128].astype(F32), 0.0), axis=1, keepdims=True
        )
        tags = jnp.sum(tag_row * tag_weight, axis=2, keepdims=True).reshape(rows, 1)
        scores_ref[pl.ds(c * rows, rows), :] = scores
        tags_ref[pl.ds(c * rows, rows), :] = tags
        most = jnp.max(scores, axis=1, keepdims=True)
        norm = jnp.log(jnp.sum(jnp.exp(scores - most), axis=1, keepdims=True)) + most
        gold = jnp.sum(jnp.where(positions == tags, scores, 0.0), axis=1, keepdims=True)
        message = jnp.sum(
            norm.reshape(group, SLOTS, 1) * norm_lane + gold.reshape(group, SLOTS, 1) * gold_lane,
            axis=1,
        )
        norm_out[pl.ds(c * group, group)] = message.reshape(group, 1, 128)
        for j in range(group):
            send(norm_out, norm_in, norm_ssem, norm_rsem, c, j)
        return 0

    lax.fori_loop(0, chunks, score, 0)

    pltpu.make_async_copy(norm_in, norm_in, norm_rsem).wait()
    received = norm_in[...].reshape(n, 128)
    norms = jnp.zeros((n, count), F32)
    golds = jnp.zeros((n, count), F32)
    place = place_ref[...]
    gold_place = gold_place_ref[...]
    for r in range(MOST):
        norms = jnp.where(place == float(r), received[:, r : r + 1], norms)
        golds = jnp.where(gold_place == float(r), received[:, 16 + r : 17 + r], golds)
    norms = jnp.where(place >= 0.0, norms, -1e30)
    most = jnp.max(norms, axis=0, keepdims=True)
    entity_norm = jnp.log(jnp.sum(jnp.exp(norms - most), axis=0, keepdims=True)) + most
    entity_gold = jnp.sum(golds, axis=0, keepdims=True)
    losses_ref[...] = cluster_loss + entity_norm - entity_gold
    total = column(entity_norm)
    total_high = total.astype(BF16).astype(F32)
    total_mid = (total - total_high).astype(BF16).astype(F32)
    total_low = total - total_high - total_mid
    total_out[...] = spread(place, (total_high, total_mid, total_low)).reshape(n, 1, 128)

    def send_totals(c, _):
        for j in range(group):
            send(total_out, total_in, total_ssem, total_rsem.at[c], c, j)
        return 0

    lax.fori_loop(0, chunks, send_totals, 0)

    total_weight = (
        (lane3 == sub3).astype(F32)
        + (lane3 == sub3 + 16).astype(F32)
        + (lane3 == sub3 + 32).astype(F32)
    )
    unused = iota((group, SLOTS, 1), 1) >= MOST
    put_high = put
    put_low = iota((rows, group), 0) == iota((rows, group), 1) * SLOTS + MOST + 1
    put_low = put_low.astype(F32).astype(BF16)

    def give_back(c, _):
        await_received(total_in, c, total_rsem.at[c])
        await_sent(snd, c, row_ssem.at[c])
        here = total_in[pl.ds(c * group, group)].reshape(group, 1, 128)
        totals = jnp.sum(here * total_weight, axis=2, keepdims=True)
        totals = jnp.where(unused, 1e30, totals).reshape(rows, 1)
        hits = (positions == tags_ref[pl.ds(c * rows, rows), :]).astype(F32)
        coef = (jnp.exp(scores_ref[pl.ds(c * rows, rows), :] - totals) - hits).astype(BF16)
        coef_ref[pl.ds(c * rows, rows), :] = coef
        returned = dot(coef, ent[...]) * inverse_root
        returned = returned + dot(put_high, parts_ref[0, pl.ds(c * group, group), :])
        returned = returned + dot(put_low, parts_ref[1, pl.ds(c * group, group), :])
        snd[pl.ds(c * group, group)] = returned.astype(BF16).reshape(group, SLOTS, width)
        for j in range(group):
            send(snd, back, back_ssem.at[c], back_rsem.at[c], c, j)
        return 0

    lax.fori_loop(0, chunks, give_back, 0)

    tile = 256

    def entity_grad(t, _):
        at = pl.ds(pl.multiple_of(t * tile, tile), tile)
        product = dot(coef_ref[:, at], rcv[...].reshape(n * SLOTS, width), TN)
        entity_grad_ref[at, :] = product * inverse_root
        return 0

    lax.fori_loop(0, ents // tile, entity_grad, 0)

    slot = iota((8, rows), 1) & (SLOTS - 1)
    carried = ((slot == MOST) | (slot == MOST + 1)).astype(F32).astype(BF16)
    centroid_grad_ref[...] = jnp.zeros_like(centroid_grad_ref)

    def collect(c, _):
        await_received(back, c, back_rsem.at[c])
        block = back[pl.ds(c * group, group)].reshape(rows, width)
        mention_grad_ref[...] += dot(chosen(c), block, TN)
        centroid_grad_ref[...] += dot(carried, block)
        return 0

    lax.fori_loop(0, chunks, collect, 0)

    def drain(c, _):
        await_sent(snd, c, back_ssem.at[c])
        return 0

    lax.fori_loop(0, chunks, drain, 0)
    for buf, sem in ((norm_out, norm_ssem), (total_out, total_ssem)):
        part = buf.at[pl.ds(1, n - 1)]
        pltpu.make_async_copy(part, part, sem).wait()


def body(n, n_gy, mentions, centroids, clusters, gold_entity, cluster_map, entities, m_state, v_state):
    count, width = mentions.shape
    ents = entities.shape[1]
    chunks = n // 16
    vmem = pl.BlockSpec(memory_space=pltpu.VMEM)
    dma = pltpu.SemaphoreType.DMA
    losses, mention_grad, centroid_grad, entity_grad = pl.pallas_call(
        functools.partial(kernel, n, n_gy),
        out_shape=(
            jax.ShapeDtypeStruct((1, count), F32),
            jax.ShapeDtypeStruct((count, width), F32),
            jax.ShapeDtypeStruct((8, width), F32),
            jax.ShapeDtypeStruct((ents, width), F32),
        ),
        in_specs=[vmem, vmem, vmem, vmem, vmem, pl.BlockSpec(memory_space=pl.ANY)],
        out_specs=(vmem, vmem, vmem, vmem),
        scratch_shapes=[
            pltpu.VMEM((ents, width), BF16),
            pltpu.VMEM((n, SLOTS, width), BF16),
            pltpu.VMEM((n, SLOTS, width), BF16),
            pltpu.VMEM((n, SLOTS, width), BF16),
            pltpu.VMEM((n * SLOTS, ents), F32),
            pltpu.VMEM((n * SLOTS, ents), BF16),
            pltpu.VMEM((n * SLOTS, 1), F32),
            pltpu.VMEM((2, n, width), BF16),
            pltpu.VMEM((n, count), F32),
            pltpu.VMEM((n, count), F32),
            pltpu.VMEM((n, 1, 128), F32),
            pltpu.VMEM((n, 1, 128), F32),
            pltpu.VMEM((n, 1, 128), F32),
            pltpu.VMEM((n, 1, 128), F32),
            dma,
            dma((chunks,)),
            dma((chunks,)),
            dma,
            dma,
            dma,
            dma((chunks,)),
            dma((chunks,)),
            dma((chunks,)),
        ],
        compiler_params=pltpu.CompilerParams(
            collective_id=0, has_side_effects=True, vmem_limit_bytes=52 << 20
        ),
        name="exchange",
    )(
        mentions,
        centroids,
        clusters,
        gold_entity.reshape(1, count),
        cluster_map.reshape(1, -1),
        entities.reshape(ents, width),
    )
    entity_grad = entity_grad.reshape(entities.shape)
    new_m = BETA_ONE * m_state + (1.0 - BETA_ONE) * entity_grad
    new_v = BETA_TWO * v_state + (1.0 - BETA_TWO) * entity_grad * entity_grad
    new_entities = (
        entities.astype(F32) - STEP_SIZE * new_m / (jnp.sqrt(new_v) + EPSILON)
    ).astype(BF16)
    return (
        losses.reshape(count),
        mention_grad,
        centroid_grad[:1],
        new_entities,
        new_m,
        new_v,
    )


def solution(mesh):
    both = ("gx", "gy")
    placed = (
        P(both, None),
        P(),
        P(both, None),
        P(both),
        P(),
        P(both, None, None),
        P(both, None, None),
        P(both, None, None),
    )
    n = mesh.shape["gx"] * mesh.shape["gy"]
    return jax.shard_map(
        functools.partial(body, n, mesh.shape["gy"]),
        mesh=mesh,
        in_specs=placed,
        out_specs=(
            P(both),
            P(both, None),
            P(both, None),
            P(both, None, None),
            P(both, None, None),
            P(both, None, None),
        ),
        check_vma=False,
    )
```

time: 448 us -> 152 us (0.34); the launches traced: 443 us -> 152 us
  waiting for transfers between devices: 219 us -> 0 us
  Pallas kernels: 0 us -> 136 us
  local copies, waits for them, and re-layouts: 101 us -> 5.91 us
  matrix products: 40.1 us -> 0 us
  starting transfers between devices: 38.4 us -> 0 us
  blocking collectives: 18.2 us -> 0 us
  between operations: 14.9 us -> 0.65 us
    unnamed x2 -> x0, waiting for transfers between devices: 158 us -> none
    pallas_call x0 -> x1, Pallas kernels: none -> 136 us  [body(): pl.pallas_call(functools.partial(kernel, n, n_gy), out_shape=(jax.ShapeDt...]
    all_to_all x5 -> x0, waiting for transfers between devices: 60.7 us -> none  [the longest x1 51.2 us: body(): lax.all_to_all(send_rows, ('gx', 'gy'), split_axis=0, concat_axis=0, tile...]
    dot_general x6 -> x0, matrix products: 40.1 us -> none  [the longest x1 20.6 us: body(): jnp.einsum('skme,skmd->ked', entity_coef, arrived, preferred_element_type...]
    all_to_all x5 -> x0, starting transfers between devices: 38.1 us -> none  [the longest x1 12.1 us: body(): lax.all_to_all(send_tags, ('gx', 'gy'), split_axis=0, concat_axis=0, tile...]
    gather x5 -> x0, local copies, waits for them, and re-layouts: 35.4 us -> none  [the longest x1 8.52 us: body(): coming_back[destinations].astype(jnp.float32)]
    scatter x4 -> x0, local copies, waits for them, and re-layouts: 34.8 us -> none  [the longest x1 21.9 us: body(): jnp.zeros((buffer_rows, width), jnp.bfloat16).at[destinations]]
    all_to_all x1 -> x0, blocking collectives: 18.2 us -> none  [body(): lax.all_to_all(total_send, ('gx', 'gy'), split_axis=0, concat_axis=0, til...]
  transfers between devices with their start and end apart: 6 -> 0, of which waited for: 4 -> 0; matrix products, arithmetic and copies ran while one was open for 12% -> 0% of each run, Pallas kernels for 0% -> 0%
where the time goes in v1:
time: 152 us
  Pallas kernels  136 us (89%)
  other arithmetic  9.53 us (6%)
  local copies, waits for them, and re-layouts  5.91 us (4%)
    pallas_call x1, Pallas kernels, body(): pl.pallas_call(functools.partial(kernel, n, n_gy), out_shape=(jax.ShapeDt...  136 us
    convert_element_type x1, other arithmetic, body(): new_entities = (entities.astype(F32) - STEP_SIZE * new_m / (jnp.sqrt(new_...  9.53 us
    unnamed x11, local copies, waits for them, and re-layouts  5.31 us

profile of v1, /device:TPU:1, one launch (start us, length us, event | category | flops | bytes accessed | tf_op | source)
XLA Modules:
  0.0 152.2 jit_solution(16234748218640990425)
XLA Ops:
  0.6 0.8 copy.14.clusters_ref
  1.4 0.0 copy-start
  1.4 0.9 copy-done
  2.4 0.0 copy-start.1
  2.4 0.9 copy-done.1
  3.3 0.0 copy-start.2
  3.3 0.7 copy-done.2
  4.0 0.0 copy-start.3
  4.0 0.7 copy-done.3
  4.6 136.1 %exchange.1 = (f32[1,128]{1,0:T(1,128)S(1)}, f32[128,1024]{1,0:T(8,128)S(1)}, f32[8,1024]{1,0:T(8,128)S(1)}, f32[1024,1024]{1,0:T(8,128)}) custom-call(bf16[128,1024]{1,0:T(8,128)(2,1)S(1)} %copy-done, bf16[128,1024]{1,0:T(8,128)(2,1)S(1)} %copy-done.1, s32[128,9]{1,0:T(8,128)S(1)} %copy.14.clusters_ref, s32[1,128]{1,0:T(1,128)S(1)} %bitcast.12, ...), custom_call_target="tpu_custom_call" | custom-call | tf_op jit(solution)/shard_map/exchange/pallas_call | solution.py:344
  140.8 0.6 slice.3
  141.4 9.5 %subtract_convert_fusion = (bf16[1,1024,1024]{2,1,0:T(8,128)(2,1)}, f32[1,1024,1024]{2,1,0:T(8,128)}, f32[1,1024,1024]{2,1,0:T(8,128)}) fusion(bf16[1,1024,1024]{2,1,0:T(8,128)(2,1)} %param.13, f32[1024,1024]{1,0:T(8,128)} %get-tuple-element.13, f32[1,1024,1024]{2,1,0:T(8,128)} %param.14, f32[1,1024,1024]{2,1,0:T(8,128)} %param.15), kind=kLoop, calls=%fused_computation.4 | loop fusion | flops 13631488 | bytes 25165824 | tf_op jit(solution)/shard_map/convert_element_type | solution.py:396
  150.9 0.5 copy.17
  151.4 0.8 copy.18
Async XLA Ops:
  1.4 0.9 copy-start
  2.4 0.9 copy-start.1
  3.3 0.7 copy-start.2
  4.0 0.7 copy-start.3

commit v2 on v1

--- a/solution.py
+++ b/solution.py
@@ -15,6 +15,8 @@
 MESH = pl.DeviceIdType.MESH
 SLOTS = 16
 MOST = 13
+TILES = 7
+SPARE = tuple((MOST + p % 3, p // 3) for p in range(MOST, 3 * TILES))
 STRIDE = 45
 F32 = jnp.float32
 BF16 = jnp.bfloat16
@@ -35,31 +37,44 @@
 def kernel(
     n,
     n_gy,
+    mentions_hbm,
+    centroids_hbm,
+    clusters_hbm,
+    gold_hbm,
+    map_hbm,
+    entities_hbm,
+    m_hbm,
+    v_hbm,
+    losses_ref,
+    mention_grad_ref,
+    centroid_grad_ref,
+    new_entities_ref,
+    new_m_ref,
+    new_v_ref,
     mentions_ref,
     centroids_ref,
     clusters_ref,
     gold_ref,
     map_ref,
-    entities_ref,
-    losses_ref,
-    mention_grad_ref,
-    centroid_grad_ref,
-    entity_grad_ref,
     ent,
     snd,
     rcv,
     back,
+    rows_ref,
     scores_ref,
     coef_ref,
     tags_ref,
+    tag_rows_ref,
     parts_ref,
+    move_ref,
+    unmove_ref,
     place_ref,
     gold_place_ref,
     norm_out,
     norm_in,
     total_out,
     total_in,
-    ent_sem,
+    in_sem,
     row_ssem,
     row_rsem,
     norm_ssem,
@@ -70,8 +85,9 @@
     back_rsem,
 ):
     count, width = mentions_ref.shape
-    ents = entities_ref.shape[0]
-    picks = clusters_ref.shape[1]
+    ents = ent.shape[0]
+    picks = clusters_ref.shape[0]
+    kept = TILES * 128
     group = 16
     chunks = n // group
     rows = group * SLOTS
@@ -85,6 +101,24 @@
         k = (i * STRIDE) & (n - 1)
         return (gx ^ lax.shift_right_logical(k, gy_bits), gy ^ (k & (n_gy - 1)))
 
+    copies = [
+        pltpu.make_async_copy(src, dst, in_sem.at[at])
+        for at, (src, dst) in enumerate(
+            (
+                (clusters_hbm, clusters_ref),
+                (gold_hbm, gold_ref),
+                (map_hbm, map_ref),
+                (mentions_hbm, mentions_ref),
+                (centroids_hbm, centroids_ref),
+                (entities_hbm, ent),
+                (m_hbm, new_m_ref),
+                (v_hbm, new_v_ref),
+            )
+        )
+    ]
+    for copy in copies[:6]:
+        copy.start()
+
     barrier = pltpu.get_barrier_semaphore()
 
     def greet(i, _):
@@ -92,8 +126,6 @@
         return 0
 
     lax.fori_loop(1, n, greet, 0)
-    ent_copy = pltpu.make_async_copy(entities_ref, ent, ent_sem)
-    ent_copy.start()
 
     def send(src, dst, ssem, rsem, c, j):
         i = c * group + j
@@ -131,18 +163,21 @@
         def _():
             await_received(buf, c, sem)
 
+    for copy in copies[:3]:
+        copy.wait()
     square = (n, n)
-    named = jnp.zeros((count, n), F32)
+    named = jnp.zeros((n, count), F32)
     for j in range(picks):
-        named = named + (clusters_ref[:, j : j + 1] == iota((count, n), 1)).astype(F32)
-    gold_named = (clusters_ref[:, 0:1] == iota((count, n), 1)).astype(F32)
+        named = named + (clusters_ref[j : j + 1, :] == iota((n, count), 0)).astype(F32)
+    gold_row = clusters_ref[0:1, :]
+    gold_named = (gold_row == iota((n, count), 0)).astype(F32)
     steps = iota(square, 0)
     partners = me ^ ((steps * STRIDE) & (n - 1))
     owner = (partners == iota(square, 1)).astype(BF16)
     row_of = (map_ref[...] == iota(square, 0)).astype(BF16)
     step_of = dot(owner, row_of).astype(BF16)
-    here = dot(step_of, named.astype(BF16), NT)
-    gold_here = dot(step_of, gold_named.astype(BF16), NT)
+    here = dot(step_of, named.astype(BF16))
+    gold_here = dot(step_of, gold_named.astype(BF16))
     earlier = (iota((count, count), 0) < iota((count, count), 1)).astype(BF16)
     rank = dot(here.astype(BF16), earlier)
     place = jnp.where(here > 0.5, rank, -1.0)
@@ -171,8 +206,7 @@
     gold_tag = column((gold_ref[...] + 1).astype(F32))
     tag_high = jnp.floor(gold_tag * (1.0 / 64.0))
     tag_low = gold_tag - 64.0 * tag_high
-    tag_rows = spread(gold_place, (tag_high, tag_low)).astype(BF16)
-    norm_out[...] = tag_rows.astype(F32).reshape(n, 1, 128)
+    tag_rows_ref[...] = spread(gold_place, (tag_high, tag_low))
 
     sub3 = iota((group, SLOTS, 128), 1)
     lane3 = iota((group, SLOTS, 128), 2)
@@ -182,31 +216,47 @@
         picked = places[:, None, :] == iota((group, SLOTS, count), 1).astype(F32)
         return picked.astype(F32).reshape(rows, count).astype(BF16)
 
-    put = iota((rows, group), 0) == iota((rows, group), 1) * SLOTS + MOST
-    put = put.astype(F32).astype(BF16)
-
-    pl.semaphore_wait(barrier, n - 1)
-
-    def send_rows(c, _):
-        block = dot(chosen(c), mentions_ref[...])
-        tags = norm_out[pl.ds(c * group, group)].reshape(group, 128).astype(BF16)
-        first = block[:, :128] + dot(put, tags)
-        slab = snd.at[pl.ds(c * group, group)]
-        slab[:, :, 0:128] = first.astype(BF16).reshape(group, SLOTS, 128)
-        slab[:, :, 128:] = block[:, 128:].astype(BF16).reshape(group, SLOTS, width - 128)
-        for j in range(group):
-            send(snd, rcv, row_ssem.at[c], row_rsem.at[c], c, j)
-        return 0
-
-    lax.fori_loop(0, chunks, send_rows, 0)
-
+    to, come = iota((rows, rows), 0), iota((rows, rows), 1)
+    for t in range((MOST + 2) // 3):
+        for ref, a, b in ((move_ref, to, come), (unmove_ref, come, to)):
+            same = (a - (a & (SLOTS - 1))) == (b - (b & (SLOTS - 1)))
+            spare_row, row = a & (SLOTS - 1), b & (SLOTS - 1)
+            fits = same & (spare_row >= MOST) & (row < MOST) & (row - 3 * t == spare_row - MOST)
+            ref[t] = fits.astype(F32).astype(BF16)
+
+    def pack(block, slab, spare):
+        tail = block[:, kept:].astype(BF16)
+        for t in range(TILES):
+            part = block[:, t * 128 : (t + 1) * 128]
+            if 3 * t < MOST:
+                part = part + dot(move_ref[t], tail)
+            part = part.reshape(group, SLOTS, 128)
+            for (row, tile), values in zip(SPARE, spare, strict=True):
+                if tile == t:
+                    part = jnp.where(sub3 == row, values.astype(F32)[:, None, :], part)
+            slab[:, :, t * 128 : (t + 1) * 128] = part.astype(BF16)
+
+    def eighth(block):
+        total = jnp.zeros((rows, 128), F32)
+        for t in range((MOST + 2) // 3):
+            total = total + dot(unmove_ref[t], block[:, t * 128 : (t + 1) * 128])
+        return total.astype(BF16)
+
+    def spare_row(block, p):
+        row, tile = SPARE[p]
+        part = block[:, :, tile * 128 : (tile + 1) * 128].astype(F32)
+        return jnp.sum(jnp.where(sub3 == row, part, 0.0), axis=1)
+
+    for copy in copies[3:5]:
+        copy.wait()
+    gold_hot = (column(gold_row.astype(F32)) == iota((count, n), 1).astype(F32)).astype(F32)
     mentions = mentions_ref[...]
     centroids = centroids_ref[...]
     cluster_scores = dot(mentions, centroids, NT) * inverse_root
     top = jnp.max(cluster_scores, axis=1, keepdims=True)
     cluster_norm = jnp.log(jnp.sum(jnp.exp(cluster_scores - top), axis=1, keepdims=True)) + top
-    cluster_gold = jnp.sum(cluster_scores * gold_named, axis=1, keepdims=True)
-    cluster_coef = (jnp.exp(cluster_scores - cluster_norm) - gold_named).astype(BF16)
+    cluster_gold = jnp.sum(cluster_scores * gold_hot, axis=1, keepdims=True)
+    cluster_coef = (jnp.exp(cluster_scores - cluster_norm) - gold_hot).astype(BF16)
     mention_grad_ref[...] = dot(cluster_coef, centroids) * inverse_root
     shares = dot(cluster_coef, mentions, TN) * inverse_root
     high = shares.astype(BF16)
@@ -214,8 +264,24 @@
     parts_ref[0] = dot(owner, high).astype(BF16)
     parts_ref[1] = dot(owner, low).astype(BF16)
     cluster_loss = as_row(cluster_norm - cluster_gold)
-
-    ent_copy.wait()
+    centroid_grad_ref[...] = jnp.zeros_like(centroid_grad_ref)
+
+    pl.semaphore_wait(barrier, n - 1)
+
+    def send_rows(c, _):
+        block = dot(chosen(c), mentions_ref[...])
+        these = pl.ds(c * group, group)
+        spare = [tag_rows_ref[these, :]]
+        spare += [parts_ref[1, these, t * 128 : (t + 1) * 128] for t in range(TILES)]
+        pack(block, snd.at[these], spare)
+        for j in range(group):
+            send(snd, rcv, row_ssem.at[c], row_rsem.at[c], c, j)
+        return 0
+
+    lax.fori_loop(0, chunks, send_rows, 0)
+    for copy in copies[6:]:
+        copy.start()
+    copies[5].wait()
 
     tag_weight = jnp.where(lane3 == sub3, 64.0, 0.0) + jnp.where(lane3 == sub3 + 16, 1.0, 0.0)
     norm_lane = (lane3 == sub3).astype(F32)
@@ -225,10 +291,14 @@
     def score(c, _):
         await_received(rcv, c, row_rsem.at[c])
         block = rcv[pl.ds(c * group, group)]
-        scores = dot(block.reshape(rows, width), ent[...], NT) * inverse_root
-        tag_row = jnp.sum(
-            jnp.where(sub3 == MOST, block[:, :, :128].astype(F32), 0.0), axis=1, keepdims=True
-        )
+        these = pl.ds(c * rows, rows)
+        rows_ref[these, 0:kept] = block.reshape(rows, kept)
+        rows_ref[these, kept:] = eighth(block.reshape(rows, kept))
+        scores = dot(rows_ref[these, :], ent[...], NT) * inverse_root
+        tag_row = spare_row(block, 0)[:, None, :]
+        for t in range(TILES):
+            at = slice(t * 128, (t + 1) * 128)
+            centroid_grad_ref[:, at] += jnp.sum(spare_row(block, t + 1), axis=0, keepdims=True)
         tags = jnp.sum(tag_row * tag_weight, axis=2, keepdims=True).reshape(rows, 1)
         scores_ref[pl.ds(c * rows, rows), :] = scores
         tags_ref[pl.ds(c * rows, rows), :] = tags
@@ -239,7 +309,9 @@
             norm.reshape(group, SLOTS, 1) * norm_lane + gold.reshape(group, SLOTS, 1) * gold_lane,
             axis=1,
         )
-        norm_out[pl.ds(c * group, group)] = message.reshape(group, 1, 128)
+        norm_out[pl.ds(c * group, group), :, 0:128] = message.reshape(group, 1, 128)
+        last = parts_ref[1, pl.ds(c * group, group), kept:].astype(F32)
+        norm_out[pl.ds(c * group, group), :, 128:256] = last.reshape(group, 1, 128)
         for j in range(group):
             send(norm_out, norm_in, norm_ssem, norm_rsem, c, j)
         return 0
@@ -247,7 +319,9 @@
     lax.fori_loop(0, chunks, score, 0)
 
     pltpu.make_async_copy(norm_in, norm_in, norm_rsem).wait()
-    received = norm_in[...].reshape(n, 128)
+    received = norm_in[:, :, 0:128].reshape(n, 128)
+    last = norm_in[:, :, 128:256].reshape(n, 128)
+    centroid_grad_ref[:, kept:] += jnp.sum(last, axis=0, keepdims=True)
     norms = jnp.zeros((n, count), F32)
     golds = jnp.zeros((n, count), F32)
     place = place_ref[...]
@@ -279,10 +353,6 @@
         + (lane3 == sub3 + 32).astype(F32)
     )
     unused = iota((group, SLOTS, 1), 1) >= MOST
-    put_high = put
-    put_low = iota((rows, group), 0) == iota((rows, group), 1) * SLOTS + MOST + 1
-    put_low = put_low.astype(F32).astype(BF16)
-
     def give_back(c, _):
         await_received(total_in, c, total_rsem.at[c])
         await_sent(snd, c, row_ssem.at[c])
@@ -293,34 +363,42 @@
         coef = (jnp.exp(scores_ref[pl.ds(c * rows, rows), :] - totals) - hits).astype(BF16)
         coef_ref[pl.ds(c * rows, rows), :] = coef
         returned = dot(coef, ent[...]) * inverse_root
-        returned = returned + dot(put_high, parts_ref[0, pl.ds(c * group, group), :])
-        returned = returned + dot(put_low, parts_ref[1, pl.ds(c * group, group), :])
-        snd[pl.ds(c * group, group)] = returned.astype(BF16).reshape(group, SLOTS, width)
+        these = pl.ds(c * group, group)
+        spare = [parts_ref[0, these, t * 128 : (t + 1) * 128] for t in range(TILES + 1)]
+        pack(returned, snd.at[these], spare)
         for j in range(group):
             send(snd, back, back_ssem.at[c], back_rsem.at[c], c, j)
         return 0
 
     lax.fori_loop(0, chunks, give_back, 0)
 
+    for copy in copies[6:]:
+        copy.wait()
     tile = 256
 
-    def entity_grad(t, _):
+    def step(t, _):
         at = pl.ds(pl.multiple_of(t * tile, tile), tile)
-        product = dot(coef_ref[:, at], rcv[...].reshape(n * SLOTS, width), TN)
-        entity_grad_ref[at, :] = product * inverse_root
-        return 0
-
-    lax.fori_loop(0, ents // tile, entity_grad, 0)
-
-    slot = iota((8, rows), 1) & (SLOTS - 1)
-    carried = ((slot == MOST) | (slot == MOST + 1)).astype(F32).astype(BF16)
-    centroid_grad_ref[...] = jnp.zeros_like(centroid_grad_ref)
+        grad = dot(coef_ref[:, at], rows_ref[...], TN) * inverse_root
+        new_m = BETA_ONE * new_m_ref[at, :] + (1.0 - BETA_ONE) * grad
+        new_v = BETA_TWO * new_v_ref[at, :] + (1.0 - BETA_TWO) * grad * grad
+        new_m_ref[at, :] = new_m
+        new_v_ref[at, :] = new_v
+        moved = ent[at, :].astype(F32) - STEP_SIZE * new_m / (jnp.sqrt(new_v) + EPSILON)
+        new_entities_ref[at, :] = moved.astype(BF16)
+        return 0
+
+    lax.fori_loop(0, ents // tile, step, 0)
 
     def collect(c, _):
         await_received(back, c, back_rsem.at[c])
-        block = back[pl.ds(c * group, group)].reshape(rows, width)
-        mention_grad_ref[...] += dot(chosen(c), block, TN)
-        centroid_grad_ref[...] += dot(carried, block)
+        block = back[pl.ds(c * group, group)]
+        flat = block.reshape(rows, kept)
+        picked = chosen(c)
+        mention_grad_ref[:, 0:kept] += dot(picked, flat, TN)
+        mention_grad_ref[:, kept:] += dot(picked, eighth(flat), TN)
+        for t in range(TILES + 1):
+            at = slice(t * 128, (t + 1) * 128)
+            centroid_grad_ref[:, at] += jnp.sum(spare_row(block, t), axis=0, keepdims=True)
         return 0
 
     lax.fori_loop(0, chunks, collect, 0)
@@ -335,38 +413,67 @@
         pltpu.make_async_copy(part, part, sem).wait()
 
 
+def store(*refs):
+    half = len(refs) // 2
+    sems = refs[-1]
+    copies = [
+        pltpu.make_async_copy(src, dst, sems.at[at])
+        for at, (src, dst) in enumerate(zip(refs[:half], refs[half:-1], strict=True))
+    ]
+    for copy in copies:
+        copy.start()
+    for copy in copies:
+        copy.wait()
+
+
 def body(n, n_gy, mentions, centroids, clusters, gold_entity, cluster_map, entities, m_state, v_state):
     count, width = mentions.shape
+    picks = clusters.shape[1]
     ents = entities.shape[1]
     chunks = n // 16
+    rows = 16 * SLOTS
+    spread = (MOST + 2) // 3
     vmem = pl.BlockSpec(memory_space=pltpu.VMEM)
+    anywhere = pl.BlockSpec(memory_space=pl.ANY)
     dma = pltpu.SemaphoreType.DMA
-    losses, mention_grad, centroid_grad, entity_grad = pl.pallas_call(
+    results = (
+        ((1, count), F32),
+        ((count, width), F32),
+        ((1, width), F32),
+        ((ents, width), BF16),
+        ((ents, width), F32),
+        ((ents, width), F32),
+    )
+    held = pl.pallas_call(
         functools.partial(kernel, n, n_gy),
-        out_shape=(
-            jax.ShapeDtypeStruct((1, count), F32),
-            jax.ShapeDtypeStruct((count, width), F32),
-            jax.ShapeDtypeStruct((8, width), F32),
-            jax.ShapeDtypeStruct((ents, width), F32),
-        ),
-        in_specs=[vmem, vmem, vmem, vmem, vmem, pl.BlockSpec(memory_space=pl.ANY)],
-        out_specs=(vmem, vmem, vmem, vmem),
+        out_shape=tuple(pltpu.VMEM(*result) for result in results),
+        in_specs=[anywhere] * 8,
+        out_specs=(vmem,) * 6,
         scratch_shapes=[
+            pltpu.VMEM((count, width), BF16),
+            pltpu.VMEM((n, width), BF16),
+            pltpu.VMEM((picks, count), jnp.int32),
+            pltpu.VMEM((1, count), jnp.int32),
+            pltpu.VMEM((1, n), jnp.int32),
             pltpu.VMEM((ents, width), BF16),
-            pltpu.VMEM((n, SLOTS, width), BF16),
-            pltpu.VMEM((n, SLOTS, width), BF16),
-            pltpu.VMEM((n, SLOTS, width), BF16),
+            pltpu.VMEM((n, SLOTS, TILES * 128), BF16),
+            pltpu.VMEM((n, SLOTS, TILES * 128), BF16),
+            pltpu.VMEM((n, SLOTS, TILES * 128), BF16),
+            pltpu.VMEM((n * SLOTS, width), BF16),
             pltpu.VMEM((n * SLOTS, ents), F32),
             pltpu.VMEM((n * SLOTS, ents), BF16),
             pltpu.VMEM((n * SLOTS, 1), F32),
+            pltpu.VMEM((n, 128), F32),
             pltpu.VMEM((2, n, width), BF16),
+            pltpu.VMEM((spread, rows, rows), BF16),
+            pltpu.VMEM((spread, rows, rows), BF16),
             pltpu.VMEM((n, count), F32),
             pltpu.VMEM((n, count), F32),
+            pltpu.VMEM((n, 1, 256), F32),
+            pltpu.VMEM((n, 1, 256), F32),
             pltpu.VMEM((n, 1, 128), F32),
             pltpu.VMEM((n, 1, 128), F32),
-            pltpu.VMEM((n, 1, 128), F32),
-            pltpu.VMEM((n, 1, 128), F32),
-            dma,
+            dma((8,)),
             dma((chunks,)),
             dma((chunks,)),
             dma,
@@ -377,30 +484,35 @@
             dma((chunks,)),
         ],
         compiler_params=pltpu.CompilerParams(
-            collective_id=0, has_side_effects=True, vmem_limit_bytes=52 << 20
+            collective_id=0, has_side_effects=True, vmem_limit_bytes=48 << 20
         ),
         name="exchange",
     )(
         mentions,
         centroids,
-        clusters,
+        clusters.T,
         gold_entity.reshape(1, count),
         cluster_map.reshape(1, -1),
         entities.reshape(ents, width),
+        m_state.reshape(ents, width),
+        v_state.reshape(ents, width),
     )
-    entity_grad = entity_grad.reshape(entities.shape)
-    new_m = BETA_ONE * m_state + (1.0 - BETA_ONE) * entity_grad
-    new_v = BETA_TWO * v_state + (1.0 - BETA_TWO) * entity_grad * entity_grad
-    new_entities = (
-        entities.astype(F32) - STEP_SIZE * new_m / (jnp.sqrt(new_v) + EPSILON)
-    ).astype(BF16)
+    losses, mention_grad, centroid_grad, new_entities, new_m, new_v = pl.pallas_call(
+        store,
+        out_shape=tuple(jax.ShapeDtypeStruct(*result) for result in results),
+        in_specs=[vmem] * 6,
+        out_specs=(anywhere,) * 6,
+        scratch_shapes=[dma((6,))],
+        compiler_params=pltpu.CompilerParams(vmem_limit_bytes=1 << 20),
+        name="store",
+    )(*(pltpu.with_memory_space_constraint(array, pltpu.VMEM) for array in held))
     return (
         losses.reshape(count),
         mention_grad,
-        centroid_grad[:1],
-        new_entities,
-        new_m,
-        new_v,
+        centroid_grad,
+        new_entities.reshape(entities.shape),
+        new_m.reshape(entities.shape),
+        new_v.reshape(entities.shape),
     )
 
 

time: 152 us -> 131 us (0.86)
  other arithmetic: 9.53 us -> 0 us
  Pallas kernels: 136 us -> 129 us
  local copies, waits for them, and re-layouts: 5.91 us -> 0 us
    convert_element_type x1 -> x0, other arithmetic: 9.53 us -> none  [body(): new_entities = (entities.astype(F32) - STEP_SIZE * new_m / (jnp.sqrt(new_...]
    pallas_call x1 -> x2, Pallas kernels: 136 us -> 129 us  [the longest x1 125 us: body(): pl.pallas_call(functools.partial(kernel, n, n_gy), out_shape=tuple((pltpu...]
    unnamed x11 -> x0, local copies, waits for them, and re-layouts: 5.31 us -> none
where the time goes in v2:
time: 131 us; the launch traced here: 130 us
  Pallas kernels  129 us (98%)
    pallas_call x1, Pallas kernels, body(): pl.pallas_call(functools.partial(kernel, n, n_gy), out_shape=tuple((pltpu...  125 us
    pallas_call x1, Pallas kernels, body(): pl.pallas_call(store, out_shape=tuple((jax.ShapeDtypeStruct(*result) for...  4.32 us

profile of v2, /device:TPU:1, one launch (start us, length us, event | category | flops | bytes accessed | tf_op | source)
XLA Modules:
  0.0 130.1 jit_solution(5634691955910084260)
XLA Ops:
  0.6 125.1 %exchange.1 = (f32[1,128]{1,0:T(1,128)S(1)}, f32[128,1024]{1,0:T(8,128)S(1)}, f32[1,1024]{1,0:T(1,128)S(1)}, bf16[1024,1024]{1,0:T(8,128)(2,1)S(1)}, f32[1024,1024]{1,0:T(8,128)S(1)}, /*index=5*/f32[1024,1024]{1,0:T(8,128)S(1)}) custom-call(bf16[128,1024]{1,0:T(8,128)(2,1)} %mentions_hbm.1, bf16[128,1024]{1,0:T(8,128)(2,1)} %centroids_hbm.1, ...), custom_call_target="tpu_custom_call" | custom-call | tf_op jit(solution)/shard_map/exchange/pallas_call | solution.py:447
  125.8 4.3 %store.1 = (f32[1,128]{1,0:T(1,128)}, f32[128,1024]{1,0:T(8,128)}, f32[1,1024]{1,0:T(1,128)}, bf16[1024,1024]{1,0:T(8,128)(2,1)}, f32[1024,1024]{1,0:T(8,128)}, /*index=5*/f32[1024,1024]{1,0:T(8,128)}) custom-call(f32[1,128]{1,0:T(1,128)S(1)} %get-tuple-element.18.refs_0_, f32[128,1024]{1,0:T(8,128)S(1)} %get-tuple-element.19.refs_1_, ...), custom_call_target="tpu_custom_call" | custom-call | tf_op jit(solution)/shard_map/store/pallas_call | solution.py:500

commit v3 on v2

--- a/solution.py
+++ b/solution.py
@@ -3,6 +3,7 @@
 
 import jax
 import jax.numpy as jnp
+import numpy as np
 from jax import lax
 from jax.experimental import pallas as pl
 from jax.experimental.pallas import tpu as pltpu
@@ -17,7 +18,11 @@
 MOST = 13
 TILES = 7
 SPARE = tuple((MOST + p % 3, p // 3) for p in range(MOST, 3 * TILES))
-STRIDE = 45
+PAIRS = ((0, 10), (9, 12), (6, 3), (11, 4), (14, 1), (8, 2), (5, 15), (13, 7))
+WORDS = tuple(
+    int(np.array(sum(pair[p] << 4 * c for c, pair in enumerate(PAIRS)), np.uint32).astype(np.int32))
+    for p in range(2)
+)
 F32 = jnp.float32
 BF16 = jnp.bfloat16
 
@@ -45,6 +50,8 @@
     entities_hbm,
     m_hbm,
     v_hbm,
+    move_hbm,
+    unmove_hbm,
     losses_ref,
     mention_grad_ref,
     centroid_grad_ref,
@@ -57,6 +64,7 @@
     gold_ref,
     map_ref,
     ent,
+    ent_t,
     snd,
     rcv,
     back,
@@ -64,23 +72,30 @@
     scores_ref,
     coef_ref,
     tags_ref,
+    names_ref,
     tag_rows_ref,
     parts_ref,
+    last_ref,
     move_ref,
     unmove_ref,
     place_ref,
     gold_place_ref,
-    norm_out,
-    norm_in,
-    total_out,
-    total_in,
+    first_out,
+    first_in,
+    gold_out,
+    gold_in,
+    second_out,
+    second_in,
+    both_out,
+    both_in,
+    third_out,
+    third_in,
     in_sem,
     row_ssem,
     row_rsem,
-    norm_ssem,
-    norm_rsem,
-    total_ssem,
-    total_rsem,
+    step_ssem,
+    step_rsem,
+    third_rsem,
     back_ssem,
     back_rsem,
 ):
@@ -97,9 +112,13 @@
     me = gx * n_gy + gy
     gy_bits = n_gy.bit_length() - 1
 
-    def partner(i):
-        k = (i * STRIDE) & (n - 1)
-        return (gx ^ lax.shift_right_logical(k, gy_bits), gy ^ (k & (n_gy - 1)))
+    def other(c, j):
+        a = lax.shift_right_logical(jnp.int32(WORDS[j & 1]), 4 * c) & (n // n_gy - 1)
+        return a, ((j // 2 * 5) & (n_gy - 1)) ^ (3 * (j & 1))
+
+    def partner(c, j):
+        a, b = other(c, j)
+        return gx ^ a, gy ^ b
 
     copies = [
         pltpu.make_async_copy(src, dst, in_sem.at[at])
@@ -111,21 +130,25 @@
                 (mentions_hbm, mentions_ref),
                 (centroids_hbm, centroids_ref),
                 (entities_hbm, ent),
+                (move_hbm, move_ref),
+                (unmove_hbm, unmove_ref),
                 (m_hbm, new_m_ref),
                 (v_hbm, new_v_ref),
             )
         )
     ]
-    for copy in copies[:6]:
+    for copy in copies[:8]:
         copy.start()
 
     barrier = pltpu.get_barrier_semaphore()
 
-    def greet(i, _):
-        pl.semaphore_signal(barrier, inc=1, device_id=partner(i), device_id_type=MESH)
-        return 0
-
-    lax.fori_loop(1, n, greet, 0)
+    def hops(k):
+        codes = (k >> 5, (k >> 3) & 3, (k >> 1) & 3, k & 1)
+        return sum((0, 1, 2, 1)[code] for code in codes)
+
+    for k in sorted(range(1, n), key=hops, reverse=True):
+        there = (gx ^ (k >> gy_bits), gy ^ (k & (n_gy - 1)))
+        pl.semaphore_signal(barrier, inc=1, device_id=there, device_id_type=MESH)
 
     def send(src, dst, ssem, rsem, c, j):
         i = c * group + j
@@ -136,7 +159,7 @@
                 dst_ref=dst.at[i],
                 send_sem=ssem,
                 recv_sem=rsem,
-                device_id=partner(i),
+                device_id=partner(c, j),
                 device_id_type=MESH,
             ).start()
 
@@ -172,7 +195,11 @@
     gold_row = clusters_ref[0:1, :]
     gold_named = (gold_row == iota((n, count), 0)).astype(F32)
     steps = iota(square, 0)
-    partners = me ^ ((steps * STRIDE) & (n - 1))
+    turn = steps & 1
+    a = jnp.where(turn == 0, WORDS[0], WORDS[1])
+    a = lax.shift_right_logical(a, 4 * lax.shift_right_logical(steps, 4)) & (n // n_gy - 1)
+    b = ((lax.shift_right_logical(steps & 15, 1) * 5) & (n_gy - 1)) ^ (3 * turn)
+    partners = me ^ (a * n_gy + b)
     owner = (partners == iota(square, 1)).astype(BF16)
     row_of = (map_ref[...] == iota(square, 0)).astype(BF16)
     step_of = dot(owner, row_of).astype(BF16)
@@ -194,19 +221,23 @@
     def as_row(col):
         return jnp.sum(jnp.where(eye, col, 0.0), axis=0, keepdims=True)
 
-    def spread(places, parts):
+    def spread(parts):
         total = jnp.zeros((n, 128), F32)
         for r in range(MOST):
-            values = jnp.zeros((count, 128), F32)
-            for p, part in enumerate(parts):
-                values = values + jnp.where(lane == 16 * p + r, part, 0.0)
-            total = total + dot((places == float(r)).astype(BF16), values.astype(BF16))
+            for places, values in parts:
+                spot = jnp.zeros((count, 128), F32)
+                for p, value in values:
+                    spot = spot + jnp.where(lane == 16 * p + r, value, 0.0)
+                total = total + dot((places == float(r)).astype(BF16), spot.astype(BF16))
         return total
 
     gold_tag = column((gold_ref[...] + 1).astype(F32))
     tag_high = jnp.floor(gold_tag * (1.0 / 64.0))
     tag_low = gold_tag - 64.0 * tag_high
-    tag_rows_ref[...] = spread(gold_place, (tag_high, tag_low))
+    names = (iota((count, 1), 0) + 1).astype(F32)
+    tag_rows_ref[...] = spread(
+        ((gold_place, ((0, tag_high), (1, tag_low))), (place, ((2, names),)))
+    )
 
     sub3 = iota((group, SLOTS, 128), 1)
     lane3 = iota((group, SLOTS, 128), 2)
@@ -215,14 +246,6 @@
         places = place_ref[pl.ds(c * group, group), :]
         picked = places[:, None, :] == iota((group, SLOTS, count), 1).astype(F32)
         return picked.astype(F32).reshape(rows, count).astype(BF16)
-
-    to, come = iota((rows, rows), 0), iota((rows, rows), 1)
-    for t in range((MOST + 2) // 3):
-        for ref, a, b in ((move_ref, to, come), (unmove_ref, come, to)):
-            same = (a - (a & (SLOTS - 1))) == (b - (b & (SLOTS - 1)))
-            spare_row, row = a & (SLOTS - 1), b & (SLOTS - 1)
-            fits = same & (spare_row >= MOST) & (row < MOST) & (row - 3 * t == spare_row - MOST)
-            ref[t] = fits.astype(F32).astype(BF16)
 
     def pack(block, slab, spare):
         tail = block[:, kept:].astype(BF16)
@@ -261,11 +284,13 @@
     shares = dot(cluster_coef, mentions, TN) * inverse_root
     high = shares.astype(BF16)
     low = (shares - high.astype(F32)).astype(BF16)
+    last_ref[...] = low[:, kept:].astype(F32)
     parts_ref[0] = dot(owner, high).astype(BF16)
     parts_ref[1] = dot(owner, low).astype(BF16)
     cluster_loss = as_row(cluster_norm - cluster_gold)
     centroid_grad_ref[...] = jnp.zeros_like(centroid_grad_ref)
 
+    copies[6].wait()
     pl.semaphore_wait(barrier, n - 1)
 
     def send_rows(c, _):
@@ -279,13 +304,34 @@
         return 0
 
     lax.fori_loop(0, chunks, send_rows, 0)
-    for copy in copies[6:]:
+    for copy in copies[8:]:
         copy.start()
     copies[5].wait()
+    copies[7].wait()
+    ent_t[...] = ent[...].T
 
     tag_weight = jnp.where(lane3 == sub3, 64.0, 0.0) + jnp.where(lane3 == sub3 + 16, 1.0, 0.0)
-    norm_lane = (lane3 == sub3).astype(F32)
-    gold_lane = (lane3 == sub3 + 16).astype(F32)
+    name_weight = (lane3 == sub3 + 32).astype(F32)
+    lane_name = (lane3 + 1).astype(F32)
+    def fill(q, _):
+        a = lax.shift_right_logical(jnp.where((q & 1) == 0, WORDS[0], WORDS[1]), 4 * (q // 2))
+        a = a & (n // n_gy - 1)
+        gold_out[q, 1] = last_ref[pl.ds(pl.multiple_of((gx ^ a) * n_gy, n_gy), n_gy), :]
+        return 0
+
+    lax.fori_loop(0, n // n_gy, fill, 0)
+
+    def along_gx(src, dst, ssem, rsem, c, turn):
+        a, _ = other(c, turn)
+        pltpu.make_async_remote_copy(
+            src_ref=src,
+            dst_ref=dst.at[2 * c + turn],
+            send_sem=ssem,
+            recv_sem=rsem,
+            device_id=(gx ^ a, gy),
+            device_id_type=MESH,
+        ).start()
+
     positions = (iota((rows, ents), 1) + 1).astype(F32)
 
     def score(c, _):
@@ -294,7 +340,7 @@
         these = pl.ds(c * rows, rows)
         rows_ref[these, 0:kept] = block.reshape(rows, kept)
         rows_ref[these, kept:] = eighth(block.reshape(rows, kept))
-        scores = dot(rows_ref[these, :], ent[...], NT) * inverse_root
+        scores = dot(rows_ref[these, :], ent_t[...]) * inverse_root
         tag_row = spare_row(block, 0)[:, None, :]
         for t in range(TILES):
             at = slice(t * 128, (t + 1) * 128)
@@ -302,62 +348,80 @@
         tags = jnp.sum(tag_row * tag_weight, axis=2, keepdims=True).reshape(rows, 1)
         scores_ref[pl.ds(c * rows, rows), :] = scores
         tags_ref[pl.ds(c * rows, rows), :] = tags
+        names = jnp.sum(tag_row * name_weight, axis=2, keepdims=True)
+        names_ref[pl.ds(c * rows, rows), :] = names.reshape(rows, 1)
         most = jnp.max(scores, axis=1, keepdims=True)
         norm = jnp.log(jnp.sum(jnp.exp(scores - most), axis=1, keepdims=True)) + most
         gold = jnp.sum(jnp.where(positions == tags, scores, 0.0), axis=1, keepdims=True)
-        message = jnp.sum(
-            norm.reshape(group, SLOTS, 1) * norm_lane + gold.reshape(group, SLOTS, 1) * gold_lane,
-            axis=1,
-        )
-        norm_out[pl.ds(c * group, group), :, 0:128] = message.reshape(group, 1, 128)
-        last = parts_ref[1, pl.ds(c * group, group), kept:].astype(F32)
-        norm_out[pl.ds(c * group, group), :, 128:256] = last.reshape(group, 1, 128)
+        mine = names == lane_name
+        norms = jnp.max(jnp.where(mine, norm.reshape(group, SLOTS, 1), -1e30), axis=1)
+        golds = jnp.sum(jnp.where(mine, gold.reshape(group, SLOTS, 1), 0.0), axis=1)
         for j in range(group):
-            send(norm_out, norm_in, norm_ssem, norm_rsem, c, j)
+            at = pl.ds(other(c, j)[1] ^ gy, 1)
+            first_out[2 * c + (j & 1), at, :] = norms[j : j + 1]
+            gold_out[2 * c + (j & 1), 0, at, :] = golds[j : j + 1]
+
+        for at, (src, dst) in enumerate(((first_out, first_in), (gold_out, gold_in))):
+
+            @pl.when(c > 0)
+            def _():
+                along_gx(src.at[2 * c], dst, step_ssem.at[at], step_rsem.at[at], c, 0)
+
+            along_gx(src.at[2 * c + 1], dst, step_ssem.at[at], step_rsem.at[at], c, 1)
         return 0
 
     lax.fori_loop(0, chunks, score, 0)
 
-    pltpu.make_async_copy(norm_in, norm_in, norm_rsem).wait()
-    received = norm_in[:, :, 0:128].reshape(n, 128)
-    last = norm_in[:, :, 128:256].reshape(n, 128)
-    centroid_grad_ref[:, kept:] += jnp.sum(last, axis=0, keepdims=True)
-    norms = jnp.zeros((n, count), F32)
-    golds = jnp.zeros((n, count), F32)
-    place = place_ref[...]
-    gold_place = gold_place_ref[...]
-    for r in range(MOST):
-        norms = jnp.where(place == float(r), received[:, r : r + 1], norms)
-        golds = jnp.where(gold_place == float(r), received[:, 16 + r : 17 + r], golds)
-    norms = jnp.where(place >= 0.0, norms, -1e30)
-    most = jnp.max(norms, axis=0, keepdims=True)
-    entity_norm = jnp.log(jnp.sum(jnp.exp(norms - most), axis=0, keepdims=True)) + most
-    entity_gold = jnp.sum(golds, axis=0, keepdims=True)
-    losses_ref[...] = cluster_loss + entity_norm - entity_gold
-    total = column(entity_norm)
-    total_high = total.astype(BF16).astype(F32)
-    total_mid = (total - total_high).astype(BF16).astype(F32)
-    total_low = total - total_high - total_mid
-    total_out[...] = spread(place, (total_high, total_mid, total_low)).reshape(n, 1, 128)
-
-    def send_totals(c, _):
+    def await_step(dst, at, sems):
+        whole = dst.at[pl.ds(1, dst.shape[0] - 1)]
+        pltpu.make_async_copy(whole, whole, sems.at[at]).wait()
+
+    def combined(norms):
+        most = functools.reduce(jnp.maximum, norms)
+        return most + jnp.log(sum(jnp.exp(norm - most) for norm in norms))
+
+    def along_gy(src, dst, at):
+        for b in range(1, n_gy):
+            pltpu.make_async_remote_copy(
+                src_ref=src,
+                dst_ref=dst.at[b],
+                send_sem=step_ssem.at[at],
+                recv_sem=step_rsem.at[at],
+                device_id=(gx, gy ^ b),
+                device_id_type=MESH,
+            ).start()
+
+    await_step(first_in, 0, step_rsem)
+    second_out[...] = combined([first_out[0]] + [first_in[q] for q in range(1, n // n_gy)])
+    along_gy(second_out, second_in, 2)
+    await_step(second_in, 2, step_rsem)
+    norm_tile = combined([second_out[...]] + [second_in[b] for b in range(1, n_gy)])
+    third_out[...] = norm_tile
+    for c in (*range(chunks - 2, chunks), *range(chunks - 2)):
+        along_gx(third_out, third_in, step_ssem.at[4], third_rsem.at[c], c, 1)
+        if c > 0:
+            along_gx(third_out, third_in, step_ssem.at[4], third_rsem.at[c], c, 0)
+        else:
+            pltpu.make_async_copy(third_out, third_in.at[0], third_rsem.at[0]).start()
+    own = iota((n_gy, count), 0) == gy
+
+    def own_row(tile):
+        return jnp.sum(jnp.where(own, tile, 0.0), axis=0, keepdims=True)
+
+    losses_ref[...] = cluster_loss + own_row(norm_tile)
+
+    unused = iota((group, SLOTS, 1), 1) >= MOST
+    def give_back(t, _):
+        c = lax.rem(t + chunks - 2, chunks)
+        pair = third_in.at[pl.ds(2 * c, 2)]
+        pltpu.make_async_copy(pair, pair, third_rsem.at[c]).wait()
+        await_sent(snd, c, row_ssem.at[c])
+        here = []
         for j in range(group):
-            send(total_out, total_in, total_ssem, total_rsem.at[c], c, j)
-        return 0
-
-    lax.fori_loop(0, chunks, send_totals, 0)
-
-    total_weight = (
-        (lane3 == sub3).astype(F32)
-        + (lane3 == sub3 + 16).astype(F32)
-        + (lane3 == sub3 + 32).astype(F32)
-    )
-    unused = iota((group, SLOTS, 1), 1) >= MOST
-    def give_back(c, _):
-        await_received(total_in, c, total_rsem.at[c])
-        await_sent(snd, c, row_ssem.at[c])
-        here = total_in[pl.ds(c * group, group)].reshape(group, 1, 128)
-        totals = jnp.sum(here * total_weight, axis=2, keepdims=True)
+            here.append(third_in[2 * c + (j & 1), pl.ds(other(c, j)[1] ^ gy, 1), :])
+        here = jnp.concatenate(here, axis=0)[:, None, :]
+        names = names_ref[pl.ds(c * rows, rows), :].reshape(group, SLOTS, 1)
+        totals = jnp.sum(jnp.where(names == lane_name, here, 0.0), axis=2, keepdims=True)
         totals = jnp.where(unused, 1e30, totals).reshape(rows, 1)
         hits = (positions == tags_ref[pl.ds(c * rows, rows), :]).astype(F32)
         coef = (jnp.exp(scores_ref[pl.ds(c * rows, rows), :] - totals) - hits).astype(BF16)
@@ -372,7 +436,11 @@
 
     lax.fori_loop(0, chunks, give_back, 0)
 
-    for copy in copies[6:]:
+    await_step(gold_in, 1, step_rsem)
+    both_out[...] = sum((gold_in[q] for q in range(1, n // n_gy)), gold_out[0])
+    along_gy(both_out, both_in, 3)
+
+    for copy in copies[8:]:
         copy.wait()
     tile = 256
 
@@ -389,7 +457,8 @@
 
     lax.fori_loop(0, ents // tile, step, 0)
 
-    def collect(c, _):
+    def collect(t, _):
+        c = lax.rem(t + chunks - 2, chunks)
         await_received(back, c, back_rsem.at[c])
         block = back[pl.ds(c * group, group)]
         flat = block.reshape(rows, kept)
@@ -403,27 +472,46 @@
 
     lax.fori_loop(0, chunks, collect, 0)
 
+    await_step(both_in, 3, step_rsem)
+    both = sum((both_in[b] for b in range(1, n_gy)), both_out[...])
+    losses_ref[...] -= own_row(both[0])
+    centroid_grad_ref[:, kept:] += own_row(both[1])
+
     def drain(c, _):
         await_sent(snd, c, back_ssem.at[c])
         return 0
 
     lax.fori_loop(0, chunks, drain, 0)
-    for buf, sem in ((norm_out, norm_ssem), (total_out, total_ssem)):
-        part = buf.at[pl.ds(1, n - 1)]
-        pltpu.make_async_copy(part, part, sem).wait()
+    for at, dst in enumerate((first_in, gold_in, second_in, both_in, third_in)):
+        await_step(dst, at, step_ssem)
 
 
 def store(*refs):
     half = len(refs) // 2
     sems = refs[-1]
+    pieces = []
+    for src, dst in zip(refs[:half], refs[half:-1], strict=True):
+        size = min(256, src.shape[0])
+        for at in range(0, src.shape[0], size):
+            pieces.append((src.at[pl.ds(at, size)], dst.at[pl.ds(at, size)]))
     copies = [
-        pltpu.make_async_copy(src, dst, sems.at[at])
-        for at, (src, dst) in enumerate(zip(refs[:half], refs[half:-1], strict=True))
+        pltpu.make_async_copy(src, dst, sems.at[at]) for at, (src, dst) in enumerate(pieces)
     ]
     for copy in copies:
         copy.start()
     for copy in copies:
         copy.wait()
+
+
+def moves():
+    spread = (MOST + 2) // 3
+    move = np.zeros((spread, 16, SLOTS, 16, SLOTS), np.float32)
+    for t in range(spread):
+        for r in range(3 * t, min(3 * t + 3, MOST)):
+            for block in range(16):
+                move[t, block, MOST + r - 3 * t, block, r] = 1.0
+    move = move.reshape(spread, 16 * SLOTS, 16 * SLOTS)
+    return jnp.asarray(move, BF16), jnp.asarray(move.transpose(0, 2, 1), BF16)
 
 
 def body(n, n_gy, mentions, centroids, clusters, gold_entity, cluster_map, entities, m_state, v_state):
@@ -447,7 +535,7 @@
     held = pl.pallas_call(
         functools.partial(kernel, n, n_gy),
         out_shape=tuple(pltpu.VMEM(*result) for result in results),
-        in_specs=[anywhere] * 8,
+        in_specs=[anywhere] * 10,
         out_specs=(vmem,) * 6,
         scratch_shapes=[
             pltpu.VMEM((count, width), BF16),
@@ -456,6 +544,7 @@
             pltpu.VMEM((1, count), jnp.int32),
             pltpu.VMEM((1, n), jnp.int32),
             pltpu.VMEM((ents, width), BF16),
+            pltpu.VMEM((width, ents), BF16),
             pltpu.VMEM((n, SLOTS, TILES * 128), BF16),
             pltpu.VMEM((n, SLOTS, TILES * 128), BF16),
             pltpu.VMEM((n, SLOTS, TILES * 128), BF16),
@@ -463,22 +552,29 @@
             pltpu.VMEM((n * SLOTS, ents), F32),
             pltpu.VMEM((n * SLOTS, ents), BF16),
             pltpu.VMEM((n * SLOTS, 1), F32),
+            pltpu.VMEM((n * SLOTS, 1), F32),
             pltpu.VMEM((n, 128), F32),
             pltpu.VMEM((2, n, width), BF16),
+            pltpu.VMEM((n, 128), F32),
             pltpu.VMEM((spread, rows, rows), BF16),
             pltpu.VMEM((spread, rows, rows), BF16),
             pltpu.VMEM((n, count), F32),
             pltpu.VMEM((n, count), F32),
-            pltpu.VMEM((n, 1, 256), F32),
-            pltpu.VMEM((n, 1, 256), F32),
-            pltpu.VMEM((n, 1, 128), F32),
-            pltpu.VMEM((n, 1, 128), F32),
-            dma((8,)),
+            pltpu.VMEM((n // n_gy, n_gy, 128), F32),
+            pltpu.VMEM((n // n_gy, n_gy, 128), F32),
+            pltpu.VMEM((n // n_gy, 2, n_gy, 128), F32),
+            pltpu.VMEM((n // n_gy, 2, n_gy, 128), F32),
+            pltpu.VMEM((n_gy, 128), F32),
+            pltpu.VMEM((n_gy, n_gy, 128), F32),
+            pltpu.VMEM((2, n_gy, 128), F32),
+            pltpu.VMEM((n_gy, 2, n_gy, 128), F32),
+            pltpu.VMEM((n_gy, 128), F32),
+            pltpu.VMEM((n // n_gy, n_gy, 128), F32),
+            dma((10,)),
             dma((chunks,)),
             dma((chunks,)),
-            dma,
-            dma,
-            dma,
+            dma((5,)),
+            dma((4,)),
             dma((chunks,)),
             dma((chunks,)),
             dma((chunks,)),
@@ -496,13 +592,14 @@
         entities.reshape(ents, width),
         m_state.reshape(ents, width),
         v_state.reshape(ents, width),
+        *moves(),
     )
     losses, mention_grad, centroid_grad, new_entities, new_m, new_v = pl.pallas_call(
         store,
         out_shape=tuple(jax.ShapeDtypeStruct(*result) for result in results),
         in_specs=[vmem] * 6,
         out_specs=(anywhere,) * 6,
-        scratch_shapes=[dma((6,))],
+        scratch_shapes=[dma((15,))],
         compiler_params=pltpu.CompilerParams(vmem_limit_bytes=1 << 20),
         name="store",
     )(*(pltpu.with_memory_space_constraint(array, pltpu.VMEM) for array in held))

time: 131 us -> 125 us (0.954)
  Pallas kernels: 129 us -> 124 us
    pallas_call x1, Pallas kernels: 125 us -> 120 us  [body(): pl.pallas_call(functools.partial(kernel, n, n_gy), out_shape=tuple((pltpu...]
where the time goes in v3:
time: 125 us; the launch traced here: 124 us
  Pallas kernels  124 us (99%)
    pallas_call x1, Pallas kernels, body(): pl.pallas_call(functools.partial(kernel, n, n_gy), out_shape=tuple((pltpu...  120 us
    pallas_call x1, Pallas kernels, body(): pl.pallas_call(store, out_shape=tuple((jax.ShapeDtypeStruct(*result) for...  4.24 us

profile of v3, /device:TPU:1, one launch (start us, length us, event | category | flops | bytes accessed | tf_op | source)
XLA Modules:
  0.0 124.4 jit_solution(15296165495577875839)
XLA Ops:
  0.6 119.5 %exchange.1 = (f32[1,128]{1,0:T(1,128)S(1)}, f32[128,1024]{1,0:T(8,128)S(1)}, f32[1,1024]{1,0:T(1,128)S(1)}, bf16[1024,1024]{1,0:T(8,128)(2,1)S(1)}, f32[1024,1024]{1,0:T(8,128)S(1)}, /*index=5*/f32[1024,1024]{1,0:T(8,128)S(1)}) custom-call(bf16[128,1024]{1,0:T(8,128)(2,1)} %mentions_hbm.1, bf16[128,1024]{1,0:T(8,128)(2,1)} %centroids_hbm.1, ...), custom_call_target="tpu_custom_call" | custom-call | tf_op jit(solution)/shard_map/exchange/pallas_call | solution.py:535
  120.2 4.2 %store.1 = (f32[1,128]{1,0:T(1,128)}, f32[128,1024]{1,0:T(8,128)}, f32[1,1024]{1,0:T(1,128)}, bf16[1024,1024]{1,0:T(8,128)(2,1)}, f32[1024,1024]{1,0:T(8,128)}, /*index=5*/f32[1024,1024]{1,0:T(8,128)}) custom-call(f32[1,128]{1,0:T(1,128)S(1)} %get-tuple-element.18.refs_0_, f32[128,1024]{1,0:T(8,128)S(1)} %get-tuple-element.19.refs_1_, ...), custom_call_target="tpu_custom_call" | custom-call | tf_op jit(solution)/shard_map/store/pallas_call | solution.py:597

commit v4 on v3

--- a/solution.py
+++ b/solution.py
@@ -260,10 +260,8 @@
             slab[:, :, t * 128 : (t + 1) * 128] = part.astype(BF16)
 
     def eighth(block):
-        total = jnp.zeros((rows, 128), F32)
-        for t in range((MOST + 2) // 3):
-            total = total + dot(unmove_ref[t], block[:, t * 128 : (t + 1) * 128])
-        return total.astype(BF16)
+        tiles = [block[:, t * 128 : (t + 1) * 128] for t in range((MOST + 2) // 3)]
+        return dot(unmove_ref[...], jnp.concatenate(tiles, axis=0)).astype(BF16)
 
     def spare_row(block, p):
         row, tile = SPARE[p]
@@ -397,7 +395,7 @@
     await_step(second_in, 2, step_rsem)
     norm_tile = combined([second_out[...]] + [second_in[b] for b in range(1, n_gy)])
     third_out[...] = norm_tile
-    for c in (*range(chunks - 2, chunks), *range(chunks - 2)):
+    for c in (chunks - 1, *range(chunks - 1)):
         along_gx(third_out, third_in, step_ssem.at[4], third_rsem.at[c], c, 1)
         if c > 0:
             along_gx(third_out, third_in, step_ssem.at[4], third_rsem.at[c], c, 0)
@@ -412,7 +410,7 @@
 
     unused = iota((group, SLOTS, 1), 1) >= MOST
     def give_back(t, _):
-        c = lax.rem(t + chunks - 2, chunks)
+        c = lax.rem(t + chunks - 1, chunks)
         pair = third_in.at[pl.ds(2 * c, 2)]
         pltpu.make_async_copy(pair, pair, third_rsem.at[c]).wait()
         await_sent(snd, c, row_ssem.at[c])
@@ -458,7 +456,7 @@
     lax.fori_loop(0, ents // tile, step, 0)
 
     def collect(t, _):
-        c = lax.rem(t + chunks - 2, chunks)
+        c = lax.rem(t + chunks - 1, chunks)
         await_received(back, c, back_rsem.at[c])
         block = back[pl.ds(c * group, group)]
         flat = block.reshape(rows, kept)
@@ -511,7 +509,7 @@
             for block in range(16):
                 move[t, block, MOST + r - 3 * t, block, r] = 1.0
     move = move.reshape(spread, 16 * SLOTS, 16 * SLOTS)
-    return jnp.asarray(move, BF16), jnp.asarray(move.transpose(0, 2, 1), BF16)
+    return jnp.asarray(move, BF16), jnp.asarray(move.transpose(2, 0, 1).reshape(16 * SLOTS, -1), BF16)
 
 
 def body(n, n_gy, mentions, centroids, clusters, gold_entity, cluster_map, entities, m_state, v_state):
@@ -557,7 +555,7 @@
             pltpu.VMEM((2, n, width), BF16),
             pltpu.VMEM((n, 128), F32),
             pltpu.VMEM((spread, rows, rows), BF16),
-            pltpu.VMEM((spread, rows, rows), BF16),
+            pltpu.VMEM((rows, spread * rows), BF16),
             pltpu.VMEM((n, count), F32),
             pltpu.VMEM((n, count), F32),
             pltpu.VMEM((n // n_gy, n_gy, 128), F32),

time: 125 us -> 125 us (level)
  no operation moved by 1% of the time
where the time goes in v4:
time: 125 us
  Pallas kernels  124 us (99%)
    pallas_call x1, Pallas kernels, body(): pl.pallas_call(functools.partial(kernel, n, n_gy), out_shape=tuple((pltpu...  120 us
    pallas_call x1, Pallas kernels, body(): pl.pallas_call(store, out_shape=tuple((jax.ShapeDtypeStruct(*result) for...  4.24 us

profile of v4, /device:TPU:1, one launch (start us, length us, event | category | flops | bytes accessed | tf_op | source)
XLA Modules:
  0.0 125.1 jit_solution(7518752119280093110)
XLA Ops:
  0.6 120.2 %exchange.1 = (f32[1,128]{1,0:T(1,128)S(1)}, f32[128,1024]{1,0:T(8,128)S(1)}, f32[1,1024]{1,0:T(1,128)S(1)}, bf16[1024,1024]{1,0:T(8,128)(2,1)S(1)}, f32[1024,1024]{1,0:T(8,128)S(1)}, /*index=5*/f32[1024,1024]{1,0:T(8,128)S(1)}) custom-call(bf16[128,1024]{1,0:T(8,128)(2,1)} %mentions_hbm.1, bf16[128,1024]{1,0:T(8,128)(2,1)} %centroids_hbm.1, ...), custom_call_target="tpu_custom_call" | custom-call | tf_op jit(solution)/shard_map/exchange/pallas_call | solution.py:533
  120.8 4.2 %store.1 = (f32[1,128]{1,0:T(1,128)}, f32[128,1024]{1,0:T(8,128)}, f32[1,1024]{1,0:T(1,128)}, bf16[1024,1024]{1,0:T(8,128)(2,1)}, f32[1024,1024]{1,0:T(8,128)}, /*index=5*/f32[1024,1024]{1,0:T(8,128)}) custom-call(f32[1,128]{1,0:T(1,128)S(1)} %get-tuple-element.18.refs_0_, f32[128,1024]{1,0:T(8,128)S(1)} %get-tuple-element.19.refs_1_, ...), custom_call_target="tpu_custom_call" | custom-call | tf_op jit(solution)/shard_map/store/pallas_call | solution.py:595
